TPU v7x, 512 devices: a whole 4x8x8 slice. The times are simulated.
512 devices in a mesh: seq: 64 (over z, x, core), tp: 8 (over y).
Axes of the slice: x: 4, y: 8, z: 8, core: 2. Of those that a mesh axis runs over, the one named last changes fastest.
Arguments:
- query: bfloat16 [8192, 8192], P('seq', 'tp'), may hold values from -1024 to 1024
- vision_kv: bfloat16 [2048, 2048], P(('seq', 'tp')), may hold values from -512 to 512
- key_gain: float32 [128], replicated, may hold values from 0.1 to 1.9
- out_grad: bfloat16 [8192, 8192], P('seq', 'tp'), may hold values from -4 to 4
- span_image: int32 [128], replicated, may hold values from 0 to 1, as said below
- span_tiles: int32 [128], replicated, may hold values from 0 to 4, as said below
Outputs:
- attn_out: bfloat16 [8192, 8192], P('seq', 'tp')
- query_grad: bfloat16 [8192, 8192], P('seq', 'tp')
- kv_grad: bfloat16 [2048, 2048], P(('seq', 'tp'))
Inputs may be any that keep to these rules, and one draw needn't show every extreme that they name: span_image never falls from one block to the next; the blocks from some block in the second half of the text on see image 1. span_tiles is zero exactly on the leading blocks before the first block that sees an image (block 0 always among them); the first block that sees each image sees all 4 of its tiles.
All inputs are finite; a program needn't handle non-finite values.
Results may differ from a plain program's by a relative error of at most 0.013.
Values may be sent and summed in bfloat16 or wider, within the bound.
No kernel may reach another device: no remote copies, remote signals or barrier semaphores. Data moves between devices by JAX's collectives and lax.ppermute only.
A program may use at most 64 MiB of HBM per device.

v0:
```python
import math

import jax
import jax.numpy as jnp
from jax import lax
from jax.sharding import PartitionSpec as P

HD = 128
BLOCK = 64
IMAGES = 2
TILES_IMG = 4


epsilon = 1e-05
neg_fill = -1e30


def row_spans(span_image, span_tiles, text_rows):
    blocks_dev = text_rows // BLOCK
    begin_block = lax.axis_index("seq") * blocks_dev
    image_dev = lax.dynamic_slice_in_dim(span_image, begin_block, blocks_dev, 0)
    tiles_dev = lax.dynamic_slice_in_dim(span_tiles, begin_block, blocks_dev, 0)
    first_tile = jnp.repeat(image_dev * TILES_IMG, BLOCK)
    last_tile = first_tile + jnp.repeat(tiles_dev, BLOCK)
    return (first_tile, last_tile)


def block_view(offset, key_span, tile_size, first_tile, last_tile):
    key_tiles = (offset + jnp.arange(key_span, dtype=jnp.int32)) // tile_size
    return (key_tiles[None, :] >= first_tile[:, None]) & (key_tiles[None, :] < last_tile[:, None])


def body(query, vision_kv, key_gain, out_grad, span_image, span_tiles):
    score_scale = 1.0 / math.sqrt(HD)
    kv_heads = lax.all_to_all(vision_kv, "tp", split_axis=1, concat_axis=0, tiled=True)
    own_rows = kv_heads.shape[0]
    heads_here = kv_heads.shape[1] // (2 * HD)
    halves = kv_heads.reshape(own_rows, heads_here, 2, HD)
    key_pre = halves[:, :, 0, :].astype(jnp.float32)
    inverse = lax.rsqrt(jnp.mean(key_pre * key_pre, axis=2, keepdims=True) + epsilon)
    normed = key_pre * inverse
    keys_own = (normed * key_gain).astype(jnp.bfloat16)
    ready_rows = jnp.stack([keys_own, halves[:, :, 1, :]], axis=2).reshape(
        own_rows, heads_here * 2 * HD
    )
    gathered = lax.all_gather(ready_rows, "seq", axis=0, tiled=True)
    vis_total = gathered.shape[0]
    kv_everyone = gathered.reshape(vis_total, heads_here, 2, HD)
    keys_all = kv_everyone[:, :, 0, :]
    values_all = kv_everyone[:, :, 1, :]
    text_rows = query.shape[0]
    group_size = query.shape[1] // (heads_here * HD)
    query_heads = query.reshape(text_rows, heads_here, group_size, HD)
    grad_heads = out_grad.reshape(text_rows, heads_here, group_size, HD)
    first_tile, last_tile = row_spans(span_image, span_tiles, text_rows)
    live_rows = last_tile > first_tile
    tile_size = vis_total // (IMAGES * TILES_IMG)
    key_block = min(256, vis_total)
    block_count = vis_total // key_block
    head_shape = (text_rows, heads_here, group_size, HD)
    stat_shape = (text_rows, heads_here, group_size)

    def scores_at(offset, key_span):
        keys_block = lax.dynamic_slice_in_dim(keys_all, offset, key_span, 0)
        raw_scores = (
            jnp.einsum(
                "rhgd,vhd->rhgv", query_heads, keys_block, preferred_element_type=jnp.float32
            )
            * score_scale
        )
        visible = block_view(offset, key_span, tile_size, first_tile, last_tile)
        return (jnp.where(visible[:, None, None, :], raw_scores, neg_fill), visible)

    def stat_step(block_idx, loop_state):
        offset = block_idx * key_block
        row_max, row_sum = loop_state
        scores, visible = scores_at(offset, key_block)
        new_max = jnp.maximum(row_max, jnp.max(scores, axis=3))
        exp_terms = jnp.where(visible[:, None, None, :], jnp.exp(scores - new_max[..., None]), 0.0)
        return (new_max, row_sum * jnp.exp(row_max - new_max) + jnp.sum(exp_terms, axis=3))

    row_max, row_sum = lax.fori_loop(
        0,
        block_count,
        stat_step,
        (jnp.full(stat_shape, neg_fill, jnp.float32), jnp.zeros(stat_shape, jnp.float32)),
    )
    row_sum = jnp.where(live_rows[:, None, None], row_sum, 1.0)
    log_total = row_max + jnp.log(row_sum)

    def out_step(block_idx, loop_state):
        offset = block_idx * key_block
        scores, visible = scores_at(offset, key_block)
        rounded = jnp.where(
            visible[:, None, None, :], jnp.exp(scores - log_total[..., None]), 0.0
        ).astype(jnp.bfloat16)
        values_block = lax.dynamic_slice_in_dim(values_all, offset, key_block, 0)
        return loop_state + jnp.einsum(
            "rhgv,vhd->rhgd", rounded, values_block, preferred_element_type=jnp.float32
        )

    out_sum = lax.fori_loop(0, block_count, out_step, jnp.zeros(head_shape, jnp.float32))
    attn_heads = out_sum.astype(jnp.bfloat16)
    attn_out = attn_heads.reshape(text_rows, heads_here * group_size * HD)
    row_delta = jnp.sum(grad_heads.astype(jnp.float32) * attn_heads.astype(jnp.float32), axis=3)

    def grads_at(offset, key_span):
        scores, visible = scores_at(offset, key_span)
        weights = jnp.where(visible[:, None, None, :], jnp.exp(scores - log_total[..., None]), 0.0)
        values_block = lax.dynamic_slice_in_dim(values_all, offset, key_span, 0)
        prob_grad = jnp.einsum(
            "rhgd,vhd->rhgv", grad_heads, values_block, preferred_element_type=jnp.float32
        )
        dscore = (weights * (prob_grad - row_delta[..., None])).astype(jnp.bfloat16)
        return (weights.astype(jnp.bfloat16), dscore)

    def key_terms(rounded, dscore, key_span):
        value_grad = jnp.einsum(
            "rhgv,rhgd->vhd", rounded, grad_heads, preferred_element_type=jnp.float32
        )
        key_grad = (
            jnp.einsum("rhgv,rhgd->vhd", dscore, query_heads, preferred_element_type=jnp.float32)
            * score_scale
        )
        return jnp.stack([key_grad, value_grad], axis=2).reshape(key_span, heads_here * 2 * HD)

    zero_query = jnp.zeros(head_shape, jnp.float32)

    def grad_step(block_idx, loop_state):
        offset = block_idx * key_block
        query_acc, term_rows = loop_state
        rounded, dscore = grads_at(offset, key_block)
        keys_block = lax.dynamic_slice_in_dim(keys_all, offset, key_block, 0)
        query_acc = query_acc + jnp.einsum(
            "rhgv,vhd->rhgd", dscore, keys_block, preferred_element_type=jnp.float32
        )
        term_block = key_terms(rounded, dscore, key_block)
        return (query_acc, lax.dynamic_update_slice_in_dim(term_rows, term_block, offset, 0))

    query_acc, term_rows = lax.fori_loop(
        0,
        block_count,
        grad_step,
        (zero_query, jnp.zeros((vis_total, heads_here * 2 * HD), jnp.float32)),
    )
    shares = lax.psum_scatter(term_rows, "seq", scatter_dimension=0, tiled=True)
    query_grad = (
        (query_acc * score_scale)
        .astype(jnp.bfloat16)
        .reshape(text_rows, heads_here * group_size * HD)
    )
    share_heads = shares.reshape(own_rows, heads_here, 2, HD)
    scaled = share_heads[:, :, 0, :] * key_gain
    pre_grad = inverse * (scaled - normed * jnp.mean(scaled * normed, axis=2, keepdims=True))
    heads_grad = (
        jnp.stack([pre_grad, share_heads[:, :, 1, :]], axis=2)
        .reshape(own_rows, heads_here * 2 * HD)
        .astype(jnp.bfloat16)
    )
    kv_grad = lax.all_to_all(heads_grad, "tp", split_axis=0, concat_axis=1, tiled=True)
    return (attn_out, query_grad, kv_grad)


def solution(mesh):
    in_specs = (P("seq", "tp"), P(("seq", "tp"), None), P(), P("seq", "tp"), P(), P())
    out_specs = (P("seq", "tp"), P("seq", "tp"), P(("seq", "tp"), None))
    return jax.shard_map(body, mesh=mesh, in_specs=in_specs, out_specs=out_specs, check_vma=False)
```

profile of v0, /device:TPU:1, one launch (start us, length us, event | category | flops | bytes accessed | tf_op | source)
XLA Modules:
  0.0 315.6 jit_solution(3581702851836055295)
XLA Ops:
  7.2 14.3 %all_to_all.32 = bf16[4,8,256]{2,0,1:T(4,128)(2,1)S(1)} all-to-all(bf16[4,8,256]{2,0,1:T(4,128)(2,1)} %bitcast.283), channel_id=1, replica_groups=mesh['seq'=64,'tp'=8] {'tp'}, dimensions={1} | all-to-all | bytes 32768 | tf_op jit(solution)/shard_map/all_to_all | solution.py:35
  21.7 0.7 fusion.76
  22.4 0.6 copy.150
  23.2 0.7 dynamic_slice.58
  24.1 0.7 dynamic-slice_multiply_fusion
  24.9 1.1 copy.108
  26.3 1.1 copy.114
  27.4 79.6 %all-gather.2.cloned.1.call-done = bf16[2048,256]{1,0:T(8,128)(2,1)} async-done(((bf16[32,256]{1,0:T(8,128)(2,1)}), bf16[2048,256]{1,0:T(8,128)(2,1)}) %all-gather.2.cloned.1.call-update) | async-done | bytes 1048592 | tf_op jit(solution)/shard_map/all_gather | solution.py:46
  107.0 1.5 copy.107
  108.9 8.2 %while.58 = (s32[]{:T(128)}, f32[128,1,8]{0,2,1:T(8,128)S(1)}, f32[128,1,8]{0,2,1:T(8,128)S(1)}, bf16[2048,1,128]{2,0,1:T(8,128)(2,1)S(1)}, bf16[128,1,8,128]{3,...) while((s32[]{:T(128)}, f32[128,1,8]{0,2,1:T(8,128)S(1)}, ...), condition=%wide.region_4.5_spmd.clone.clone.clone, body=%wide.region_1.4_spmd.clone.clone.clone.sunk | while | flops 68789384 | bytes 2584262 | solution.py:82
  117.1 8.6 %while.59 = (s32[]{:T(128)}, f32[128,1,8,128]{0,3,2,1:T(8,128)S(1)}, bf16[2048,1,128]{0,2,1:T(8,128)(2,1)S(1)}, bf16[2048,1,128]{2,0,1:T(8,128)(2,1)S(1)}, bf16[...) while((s32[]{:T(128)}, ...), condition=%wide.region_6.7_spmd.clone.clone.clone, body=%wide.region_5.6_spmd.clone.clone.clone.sunk | while | flops 135893120 | bytes 1520840 | solution.py:102
  117.6 0.6 fusion.110
  118.7 0.6 fusion.110
  119.7 0.6 fusion.110
  120.8 0.6 fusion.110
  121.9 0.6 fusion.110
  122.9 0.6 fusion.110
  124.0 0.6 fusion.110
  125.1 0.6 fusion.110
  125.8 1.5 broadcast_in_dim.204.clone
  127.3 24.3 %while.60 = (s32[]{:T(128)}, f32[128,1,8,128]{0,3,2,1:T(8,128)S(1)}, f32[2048,256]{1,0:T(8,128)}, bf16[2048,1,128]{2,0,1:T(8,128)(2,1)S(1)}, bf16[128,1,8,128]{0...) while((s32[]{:T(128)}, ...), condition=%wide.region_9.10_spmd.clone.clone.clone, body=%wide.region_8.9_spmd.clone.clone.clone.sunk | while | flops 338104448 | bytes 8929009 | solution.py:140
  127.7 0.4 fusion.121
  129.6 0.7 constant_dynamic-update-slice_fusion.2
  130.7 0.4 fusion.121
  132.6 0.7 constant_dynamic-update-slice_fusion.2
  133.7 0.4 fusion.121
  134.5 0.3 fusion.122
  135.6 0.7 constant_dynamic-update-slice_fusion.2
  136.8 0.4 fusion.121
  137.5 0.3 fusion.122
  138.6 0.7 constant_dynamic-update-slice_fusion.2
  139.8 0.4 fusion.121
  141.7 0.7 constant_dynamic-update-slice_fusion.2
  142.8 0.4 fusion.121
  143.6 0.3 fusion.122
  144.7 0.7 constant_dynamic-update-slice_fusion.2
  145.9 0.4 fusion.121
  147.8 0.7 constant_dynamic-update-slice_fusion.2
  148.9 0.4 fusion.121
  150.8 0.7 constant_dynamic-update-slice_fusion.2
  151.6 141.5 %reduce-scatter.4.cloned.1.call-done = f32[32,256]{1,0:T(8,128)} async-done(((f32[2048,256]{1,0:T(8,128)}), f32[32,256]{1,0:T(8,128)}) %reduce-scatter.4.cloned.1.call-update) | async-done | bytes 32784
  293.1 0.9 copy.136
  294.4 0.6 convert_element_type.93
  295.0 6.5 %all-to-all-start.1 = ((bf16[8,4,256]{2,1,0:T(4,128)(2,1)}), bf16[8,4,256]{2,1,0:T(4,128)(2,1)S(1)}, u32[]{:S(2)}, u32[]{:S(2)}) async-start(bf16[8,4,256]{2,1,0:T(4,128)(2,1)} %convert_element_type.93), calls=%async_computation.1 | async-start | bytes 32768 | tf_op jit(solution)/shard_map/all_to_all | solution.py:160
  301.6 0.9 copy.129
  302.4 0.8 copy.130
  303.3 4.9 %all-to-all-done.1 = bf16[8,4,256]{2,1,0:T(4,128)(2,1)S(1)} async-done(((bf16[8,4,256]{2,1,0:T(4,128)(2,1)}), bf16[8,4,256]{2,1,0:T(4,128)(2,1)S(1)}, u32[]{:S(2)}, u32[]{:S(2)}) %all-to-all-start.1) | async-done | bytes 16416 | tf_op jit(solution)/shard_map/all_to_all | solution.py:160
  308.1 0.6 copy.179
  (292 shorter events, 26.6 us)
Async XLA Ops:
  7.2 99.9 %all-gather.2.cloned.1.call-start = ((), (), s32[]{:S(2)}) async-start(), calls=%async_computation.3 | async-start | bytes 1064960 | tf_op jit(solution)/shard_map/all_gather | solution.py:46
  23.1 270.0 %reduce-scatter.4.cloned.1.call-start = ((), (), s32[]{:S(2)}) async-start(), calls=%async_computation.4 | async-start | bytes 2129920
  108.9 8.2 %copy-start = (f32[128,1,8,128]{0,3,2,1:T(8,128)S(1)}, f32[128,1,8,128]{0,3,2,1:T(8,128)}, u32[]{:S(2)}) copy-start(f32[128,1,8,128]{0,3,2,1:T(8,128)} %custom-call.2) | copy-start | bytes 1572868
  151.5 142.5 %copy-start.1 = (f32[128]{0:T(128)S(1)}, f32[128]{0:T(128)}, u32[]{:S(2)}) copy-start(f32[128]{0:T(128)} %param.14) | copy-start | bytes 1540
  295.0 13.1 %all-to-all-start.1 = ((bf16[8,4,256]{2,1,0:T(4,128)(2,1)}), bf16[8,4,256]{2,1,0:T(4,128)(2,1)S(1)}, u32[]{:S(2)}, u32[]{:S(2)}) async-start(bf16[8,4,256]{2,1,0:T(4,128)(2,1)} %convert_element_type.93), calls=%async_computation.1 | async-start | bytes 32768 | tf_op jit(solution)/shard_map/all_to_all | solution.py:160
Sparse Core Ops, SparseCore 0:
  23.2 83.7 all-gather.1
  151.7 141.3 reduce-scatter.3
where the time goes:
time: 321 us; the launch traced here: 316 us
  waiting for transfers between devices  226 us (70%)
  local copies, waits for them, and re-layouts  25.7 us (8%)
  matrix products  20.6 us (6%)
  blocking collectives  14.3 us (4%)
  between operations  14.2 us (4%)
  other arithmetic  6.73 us (2%)
  starting transfers between devices  6.56 us (2%)
    unnamed x3, waiting for transfers between devices  142 us
    all_gather x1, waiting for transfers between devices, body(): gathered = lax.all_gather(ready_rows, 'seq', axis=0, tiled=True)  79.6 us
    all_to_all x1, blocking collectives, body(): lax.all_to_all(vision_kv, 'tp', split_axis=1, concat_axis=0, tiled=True)  14.3 us
    dynamic_update_slice x16, local copies, waits for them, and re-layouts, grad_step(): lax.dynamic_update_slice_in_dim(term_rows, term_block, offset, 0)  6.84 us
    all_to_all x1, starting transfers between devices, body(): lax.all_to_all(heads_grad, 'tp', split_axis=0, concat_axis=1, tiled=True)  6.48 us
  transfers between devices with their start and end apart: 3, of which 3 were waited for; matrix products, arithmetic and copies ran while one was open for 2% of the time, Pallas kernels for 0%

commit v1 on v0

v1 whole, which is shorter than its diff:
```python
import functools
import math

import jax
import jax.numpy as jnp
from jax import lax
from jax.experimental import pallas as pl
from jax.experimental.pallas import tpu as pltpu
from jax.sharding import Mesh, PartitionSpec as P

HD = 128
BLOCK = 64
TILES_IMG = 4

epsilon = 1e-05
neg_fill = -1e30
score_scale = 1.0 / math.sqrt(HD)

NN = (((1,), (0,)), ((), ()))
NT = (((1,), (1,)), ((), ()))
TN = (((0,), (0,)), ((), ()))


def dot(a, b, dims):
    return lax.dot_general(a, b, dims, preferred_element_type=jnp.float32)


def attention_kernel(
    seq_index, image_ref, tiles_ref, gain_ref, query_ref, grad_ref, kv_ref,
    out_ref, query_grad_ref, terms_ref, keys_ref, values_ref, key_acc, value_acc,
):
    groups, group_rows, _ = kv_ref.shape
    image_rows = group_rows // 2
    part = image_rows // TILES_IMG
    span = groups * image_rows
    heads = query_ref.shape[1] // HD
    begin = seq_index() * 2
    image_a, image_b = image_ref[begin], image_ref[begin + 1]
    tiles_a, tiles_b = tiles_ref[begin], tiles_ref[begin + 1]
    column = lax.broadcasted_iota(jnp.int32, (1, span), 1)
    column_tile = lax.rem(lax.div(column, part), TILES_IMG)

    def image_slice(image):
        return pl.ds(pl.multiple_of(image * image_rows, image_rows), image_rows)

    def load_image(image):
        rows = image_slice(image)
        pre = kv_ref[:, rows, :HD].astype(jnp.float32).reshape(span, HD)
        inverse = lax.rsqrt(jnp.mean(pre * pre, axis=1, keepdims=True) + epsilon)
        keys_ref[...] = (pre * inverse * gain_ref[...]).astype(jnp.bfloat16)
        values_ref[...] = kv_ref[:, rows, HD:].reshape(span, HD)

    def stacked(ref, row, first, count):
        return jnp.concatenate(
            [ref[row : row + BLOCK, j * HD : (j + 1) * HD] for j in range(first, first + count)], axis=0
        )

    def unstack(ref, row, first, count, rows):
        for j in range(count):
            ref[row : row + BLOCK, (first + j) * HD : (first + j + 1) * HD] = rows[j * BLOCK : (j + 1) * BLOCK]

    per_chunk = 4

    def block_step(row, tiles, fresh):
        bias = jnp.where(column_tile < tiles, 0.0, neg_fill)
        live = (tiles > 0).astype(jnp.float32)
        for first in range(0, heads, per_chunk):
            query = stacked(query_ref, row, first, per_chunk)
            grad = stacked(grad_ref, row, first, per_chunk)
            scores = dot(query, keys_ref[...], NT) + bias
            row_max = jnp.max(scores, axis=1, keepdims=True)
            terms = jnp.exp((scores - row_max) * score_scale)
            inverse_sum = live / jnp.sum(terms, axis=1, keepdims=True)
            weights = terms * inverse_sum
            probs = weights.astype(jnp.bfloat16)
            out = dot(probs, values_ref[...], NN).astype(jnp.bfloat16)
            unstack(out_ref, row, first, per_chunk, out)
            delta = jnp.sum(grad.astype(jnp.float32) * out.astype(jnp.float32), axis=1, keepdims=True)
            prob_grad = dot(grad, values_ref[...], NT)
            dscore = (weights * (prob_grad - delta)).astype(jnp.bfloat16)
            query_grad = (dot(dscore, keys_ref[...], NN) * score_scale).astype(jnp.bfloat16)
            unstack(query_grad_ref, row, first, per_chunk, query_grad)
            value_term = dot(probs, grad, TN)
            key_term = dot(dscore, query, TN)
            if fresh and first == 0:
                value_acc[...] = value_term
                key_acc[...] = key_term
            else:
                value_acc[...] += value_term
                key_acc[...] += key_term

    def store_terms(image):
        rows = image_slice(image)
        terms_ref[:, rows, :HD] = (
            (key_acc[...] * score_scale).astype(jnp.bfloat16).reshape(groups, image_rows, HD)
        )
        terms_ref[:, rows, HD:] = value_acc[...].astype(jnp.bfloat16).reshape(groups, image_rows, HD)

    load_image(image_a)
    block_step(0, tiles_a, True)

    @pl.when(image_a == image_b)
    def _():
        terms_ref[:, image_slice(1 - image_a), :] = jnp.zeros((groups, image_rows, 2 * HD), jnp.bfloat16)

    @pl.when(image_a != image_b)
    def _():
        store_terms(image_a)
        load_image(image_b)
        value_acc[...] = jnp.zeros_like(value_acc)
        key_acc[...] = jnp.zeros_like(key_acc)

    block_step(BLOCK, tiles_b, False)
    store_terms(image_b)


def attention(seq_index, span_image, span_tiles, key_gain, query, out_grad, kv):
    groups, group_rows, _ = kv.shape
    span = groups * group_rows // 2
    vmem = pl.BlockSpec(memory_space=pltpu.VMEM)
    smem = pl.BlockSpec(memory_space=pltpu.SMEM)
    work = 6 * 2 * query.size * span
    return pl.pallas_call(
        functools.partial(attention_kernel, seq_index),
        out_shape=[
            jax.ShapeDtypeStruct(query.shape, jnp.bfloat16),
            jax.ShapeDtypeStruct(query.shape, jnp.bfloat16),
            jax.ShapeDtypeStruct(kv.shape, jnp.bfloat16),
        ],
        in_specs=[smem, smem, vmem, vmem, vmem, vmem],
        out_specs=[vmem, vmem, vmem],
        scratch_shapes=[
            pltpu.VMEM((span, HD), jnp.bfloat16),
            pltpu.VMEM((span, HD), jnp.bfloat16),
            pltpu.VMEM((span, HD), jnp.float32),
            pltpu.VMEM((span, HD), jnp.float32),
        ],
        compiler_params=pltpu.CompilerParams(vmem_limit_bytes=40 * 1024 * 1024),
        cost_estimate=pl.CostEstimate(flops=work, bytes_accessed=5 * 1024 * 1024, transcendentals=query.size * span // HD),
        name="attention",
    )(span_image, span_tiles, key_gain, query, out_grad, kv)


def spread(rows, axes, copies):
    return lax.all_to_all(
        lax.optimization_barrier(jnp.broadcast_to(rows, (copies,) + rows.shape)), axes, split_axis=0, concat_axis=0
    )


def body(query, vision_kv, key_gain, out_grad, span_image, span_tiles):
    z, x, cores, tp = (lax.axis_size(name) for name in ("z", "x", "c", "tp"))
    own_rows = vision_kv.shape[0]
    share_rows = own_rows * tp

    by_head = vision_kv.reshape(own_rows, tp, 2 * HD).transpose(1, 0, 2)
    copies = lax.optimization_barrier(jnp.broadcast_to(by_head, (z,) + by_head.shape))
    along_z = lax.all_to_all(
        copies.reshape(z * tp, own_rows, 2 * HD), ("z", "tp"), split_axis=0, concat_axis=0, tiled=True
    )
    column = along_z.reshape(z * share_rows, 2 * HD)
    plane = spread(column, "x", x)
    kv = spread(plane, "c", cores).reshape(cores * x, z * share_rows, 2 * HD)

    def seq_index():
        return (lax.axis_index("z") * x + lax.axis_index("x")) * cores + lax.axis_index("c")

    attn_out, query_grad, terms = attention(
        seq_index, span_image, span_tiles, key_gain.reshape(1, HD), query, out_grad, kv
    )

    def fold(terms, axis, parts):
        got = lax.all_to_all(
            terms.reshape((parts, -1) + terms.shape[1:]), axis, split_axis=0, concat_axis=0
        )
        return jnp.sum(got.astype(jnp.float32), axis=0).astype(jnp.bfloat16)

    terms = fold(terms, "c", cores)
    terms = fold(terms, "x", x)
    got = lax.all_to_all(
        terms.reshape(z * tp, own_rows, 2 * HD), ("z", "tp"), split_axis=0, concat_axis=0, tiled=True
    )
    shares = jnp.sum(got.reshape(z, tp, own_rows, 2, HD).astype(jnp.float32), axis=0)

    halves = by_head.reshape(tp, own_rows, 2, HD)
    key_pre = halves[:, :, 0].astype(jnp.float32)
    inverse = lax.rsqrt(jnp.mean(key_pre * key_pre, axis=2, keepdims=True) + epsilon)
    normed = key_pre * inverse
    scaled = shares[:, :, 0] * key_gain
    pre_grad = inverse * (scaled - normed * jnp.mean(scaled * normed, axis=2, keepdims=True))
    kv_grad = jnp.stack([pre_grad, shares[:, :, 1]], axis=2).astype(jnp.bfloat16)
    kv_grad = kv_grad.reshape(tp, own_rows, 2 * HD).transpose(1, 0, 2).reshape(own_rows, tp * 2 * HD)
    return (attn_out, query_grad, kv_grad)


def solution(mesh):
    fine = Mesh(mesh.devices.reshape(8, 4, 2, 8), ("z", "x", "c", "tp"))
    seq = ("z", "x", "c")
    in_specs = (P(seq, "tp"), P(seq + ("tp",), None), P(), P(seq, "tp"), P(), P())
    out_specs = (P(seq, "tp"), P(seq, "tp"), P(seq + ("tp",), None))
    return jax.shard_map(body, mesh=fine, in_specs=in_specs, out_specs=out_specs, check_vma=False)
```

time: 321 us -> 91.1 us (0.28); the launches traced: 316 us -> 90.7 us
  waiting for transfers between devices: 226 us -> 11.5 us
  blocking collectives: 14.3 us -> 63.3 us
  local copies, waits for them, and re-layouts: 25.7 us -> 3.06 us
  matrix products: 20.6 us -> 0 us
  between operations: 14.2 us -> 0.75 us
  Pallas kernels: 0 us -> 6.41 us
  other arithmetic: 6.73 us -> 1.01 us
    unnamed x3 -> x0, waiting for transfers between devices: 142 us -> none
    all_gather x1 -> x0, waiting for transfers between devices: 79.6 us -> none  [body(): gathered = lax.all_gather(ready_rows, 'seq', axis=0, tiled=True)]
    all_to_all x1 -> x5, blocking collectives: 14.3 us -> 63.3 us  [the longest x1 28.5 us: body(): lax.all_to_all(copies.reshape(z * tp, own_rows, 2 * HD), ('z', 'tp'), spl...]
    dot_general x56 -> x0, matrix products: 20.6 us -> none  [the longest x16 5.62 us: scores_at(): jnp.einsum('rhgd,vhd->rhgv', query_heads, keys_block, preferred_element_t...]
    dynamic_update_slice x16 -> x0, local copies, waits for them, and re-layouts: 6.84 us -> none  [grad_step(): lax.dynamic_update_slice_in_dim(term_rows, term_block, offset, 0)]
    all_to_all x1, waiting for transfers between devices: 4.86 us -> 11.5 us  [body(): lax.all_to_all(terms.reshape(z * tp, own_rows, 2 * HD), ('z', 'tp'), spli...]
    pallas_call x0 -> x1, Pallas kernels: none -> 6.41 us  [attention(): pl.pallas_call(functools.partial(attention_kernel, seq_index), out_shape=...]
    broadcast_in_dim x51 -> x3, local copies, waits for them, and re-layouts: 4.96 us -> 0.14 us  [the longest x2 0.1 us: spread(): jnp.broadcast_to(rows, (copies,) + rows.shape)]
  transfers between devices with their start and end apart: 3 -> 1, of which waited for: 3 -> 1; matrix products, arithmetic and copies ran while one was open for 2% -> 0% of each run, Pallas kernels for 0% -> 0%
where the time goes in v1:
time: 91.1 us; the launch traced here: 90.7 us
  blocking collectives  63.3 us (69%)
  waiting for transfers between devices  11.5 us (13%)
  Pallas kernels  6.41 us (7%)
  starting transfers between devices  4.62 us (5%)
  local copies, waits for them, and re-layouts  3.06 us (3%)
  other arithmetic  1.01 us (1%)
    all_to_all x1, blocking collectives, body(): lax.all_to_all(copies.reshape(z * tp, own_rows, 2 * HD), ('z', 'tp'), spl...  28.5 us
    all_to_all x2, blocking collectives, spread(): lax.all_to_all(lax.optimization_barrier(jnp.broadcast_to(rows, (copies,)...  18.6 us
    all_to_all x2, blocking collectives, fold(): lax.all_to_all(terms.reshape((parts, -1) + terms.shape[1:]), axis, split_...  16.2 us
    all_to_all x1, waiting for transfers between devices, body(): lax.all_to_all(terms.reshape(z * tp, own_rows, 2 * HD), ('z', 'tp'), spli...  11.5 us
    pallas_call x1, Pallas kernels, attention(): pl.pallas_call(functools.partial(attention_kernel, seq_index), out_shape=...  6.41 us
    all_to_all x1, starting transfers between devices, body(): lax.all_to_all(terms.reshape(z * tp, own_rows, 2 * HD), ('z', 'tp'), spli...  4.62 us
    unnamed x13, local copies, waits for them, and re-layouts  2.03 us
  transfers between devices with their start and end apart: 1, of which 1 were waited for; matrix products, arithmetic and copies ran while one was open for 0% of the time, Pallas kernels for 0%

profile of v1, /device:TPU:1, one launch (start us, length us, event | category | flops | bytes accessed | tf_op | source)
XLA Modules:
  0.0 90.7 jit_solution(5097479203726031676)
XLA Ops:
  0.6 0.7 copy.53
  1.4 28.5 %all_to_all.30 = bf16[64,4,256]{2,1,0:T(4,128)(2,1)S(1)} all-to-all(bf16[64,4,256]{2,1,0:T(4,128)(2,1)S(1)} %bitcast.55), channel_id=1, replica_groups=mesh['z'=8,'x'=4,'c'=2,'tp'=8] {'z','tp'}, dimensions={0} | all-to-all | bytes 262144 | tf_op jit(solution)/shard_map/all_to_all | solution.py:157
  30.0 10.8 %all_to_all.31 = bf16[4,256,256]{2,1,0:T(8,128)(2,1)S(1)} all-to-all(bf16[4,256,256]{2,1,0:T(8,128)(2,1)S(1)} %broadcast_in_dim.13), channel_id=1, replica_groups=mesh['z'=8,'x'=4,'c'=2,'tp'=8] {'x'}, dimensions={0} | all-to-all | bytes 1048576 | tf_op jit(solution)/shard_map/all_to_all | solution.py:145
  40.7 0.1 broadcast_in_dim.14
  40.8 0.0 copy-start.1
  40.8 0.0 copy-start.2
  40.8 7.9 %all_to_all.32 = bf16[2,4,256,256]{3,2,1,0:T(8,128)(2,1)S(1)} all-to-all(bf16[2,4,256,256]{3,2,1,0:T(8,128)(2,1)S(1)} %broadcast_in_dim.14), channel_id=1, replica_groups=mesh['z'=8,'x'=4,'c'=2,'tp'=8] {'c'}, dimensions={0} | all-to-all | bytes 2097152 | tf_op jit(solution)/shard_map/all_to_all | solution.py:145
  48.7 0.0 copy-start
  48.7 0.0 copy-start.3
  48.7 0.0 copy-start.4
  48.7 0.0 copy-done.1
  48.7 0.0 copy-done.2
  48.7 0.6 copy-done
  49.4 0.0 copy-done.3
  49.4 0.0 copy-done.4
  49.4 6.4 %attention.1 = (bf16[128,1024]{1,0:T(8,128)(2,1)}, bf16[128,1024]{1,0:T(8,128)(2,1)}, bf16[8,256,256]{2,1,0:T(8,128)(2,1)S(1)}) custom-call(s32[128]{0:T(128)S(1)} %copy-done.3, s32[128]{0:T(128)S(1)} %copy-done.4, f32[1,128]{1,0:T(1,128)S(1)} %bitcast.53, bf16[128,1024]{1,0:T(8,128)(2,1)S(1)} %copy-done.1, bf16[128,1024]{1,0:T(8,128)(2,1)S(1)} %copy-done.2, ...), custom_call_target="tpu_custom_call" | custom-call | flops 1610612736 | bytes 5242880 | tf_op jit(solution)/shard_map/attention/pallas_call | solution.py:123
  55.8 4.6 %all_to_all.33 = bf16[2,4,256,256]{3,2,1,0:T(8,128)(2,1)S(1)} all-to-all(bf16[2,4,256,256]{3,2,1,0:T(8,128)(2,1)S(1)} %bitcast.52), channel_id=1, replica_groups=mesh['z'=8,'x'=4,'c'=2,'tp'=8] {'c'}, dimensions={0} | all-to-all | bytes 2097152 | tf_op jit(solution)/shard_map/all_to_all | solution.py:172
  60.4 0.5 reduce_sum.52
  60.8 11.6 %all_to_all.34 = bf16[4,1,256,256]{3,2,1,0:T(8,128)(2,1)S(1)} all-to-all(bf16[4,1,256,256]{3,2,1,0:T(8,128)(2,1)S(1)} %bitcast.54), channel_id=1, replica_groups=mesh['z'=8,'x'=4,'c'=2,'tp'=8] {'x'}, dimensions={0} | all-to-all | bytes 1048576 | tf_op jit(solution)/shard_map/all_to_all | solution.py:172
  72.5 0.1 reduce_sum.53
  72.5 0.7 reshape.67
  73.2 4.6 %all-to-all-start.5 = ((bf16[64,4,256]{2,1,0:T(4,128)(2,1)}), bf16[64,4,256]{2,1,0:T(4,128)(2,1)S(1)}, u32[]{:S(2)}, u32[]{:S(2)}) async-start(bf16[64,4,256]{2,1,0:T(4,128)(2,1)} %reshape.67), calls=%async_computation.5 | async-start | bytes 262144 | tf_op jit(solution)/shard_map/all_to_all | solution.py:179
  77.8 0.1 fusion.2
  77.9 11.5 %all-to-all-done.5 = bf16[64,4,256]{2,1,0:T(4,128)(2,1)S(1)} async-done(((bf16[64,4,256]{2,1,0:T(4,128)(2,1)}), bf16[64,4,256]{2,1,0:T(4,128)(2,1)S(1)}, u32[]{:S(2)}, u32[]{:S(2)}) %all-to-all-start.5) | async-done | bytes 131104 | tf_op jit(solution)/shard_map/all_to_all | solution.py:179
  89.5 0.1 reshape.70
  89.7 0.1 reduce_sum.54
  89.8 0.2 fusion.4
  90.0 0.1 fusion.8
  90.1 0.6 copy.45
  (11 shorter events, 0.2 us)
Async XLA Ops:
  40.8 7.9 %copy-start.1 = (bf16[128,1024]{1,0:T(8,128)(2,1)S(1)}, bf16[128,1024]{1,0:T(8,128)(2,1)}, u32[]{:S(2)}) copy-start(bf16[128,1024]{1,0:T(8,128)(2,1)} %query_ref.1) | copy-start | bytes 786436
  40.8 7.9 %copy-start.2 = (bf16[128,1024]{1,0:T(8,128)(2,1)S(1)}, bf16[128,1024]{1,0:T(8,128)(2,1)}, u32[]{:S(2)}) copy-start(bf16[128,1024]{1,0:T(8,128)(2,1)} %grad_ref.1) | copy-start | bytes 786436
  48.7 0.7 copy-start
  48.7 0.7 copy-start.3
  48.7 0.7 copy-start.4
  73.2 16.3 %all-to-all-start.5 = ((bf16[64,4,256]{2,1,0:T(4,128)(2,1)}), bf16[64,4,256]{2,1,0:T(4,128)(2,1)S(1)}, u32[]{:S(2)}, u32[]{:S(2)}) async-start(bf16[64,4,256]{2,1,0:T(4,128)(2,1)} %reshape.67), calls=%async_computation.5 | async-start | bytes 262144 | tf_op jit(solution)/shard_map/all_to_all | solution.py:179

commit v2 on v1

v2 whole, which is shorter than its diff:
```python
import functools
import math

import jax
import jax.numpy as jnp
from jax import lax
from jax.experimental import pallas as pl
from jax.experimental.pallas import tpu as pltpu
from jax.sharding import Mesh, PartitionSpec as P

HD = 128
BLOCK = 64
TILES_IMG = 4

epsilon = 1e-05
neg_fill = -1e30
score_scale = 1.0 / math.sqrt(HD)

NN = (((1,), (0,)), ((), ()))
NT = (((1,), (1,)), ((), ()))
TN = (((0,), (0,)), ((), ()))


def dot(a, b, dims):
    return lax.dot_general(a, b, dims, preferred_element_type=jnp.float32)


def attention_kernel(
    info_ref, query_ref, grad_ref, kv_ref, out_ref, query_grad_ref, terms_ref, keys_ref, values_ref, key_acc, value_acc,
):
    groups, group_rows, _ = kv_ref.shape
    image_rows = group_rows // 2
    part = image_rows // TILES_IMG
    span = groups * image_rows
    heads = query_ref.shape[1] // HD
    lane = lax.broadcasted_iota(jnp.int32, info_ref.shape, 1)
    images, tiles = (
        [jnp.sum(jnp.where(lane == k, info_ref[...], 0.0)).astype(jnp.int32) for k in pair] for pair in ((0, 1), (2, 3))
    )
    mixed = images[0] != images[1]
    slots = [0, mixed.astype(jnp.int32)]

    def image_slice(image):
        return pl.ds(pl.multiple_of(image * image_rows, image_rows), image_rows)

    def load_image(slot, image):
        rows = image_slice(image)
        keys_ref[slot] = kv_ref[:, rows, :HD].reshape(span, HD)
        values_ref[slot] = kv_ref[:, rows, HD:].reshape(span, HD)

    def stacked(ref, row, first, count):
        return jnp.concatenate(
            [ref[row : row + BLOCK, j * HD : (j + 1) * HD] for j in range(first, first + count)], axis=0
        )

    def unstack(ref, row, first, count, rows):
        for j in range(count):
            ref[row : row + BLOCK, (first + j) * HD : (first + j + 1) * HD] = rows[j * BLOCK : (j + 1) * BLOCK]

    per_chunk = 4
    column = lax.broadcasted_iota(jnp.int32, (1, span), 1)
    column_tile = lax.rem(lax.div(column, part), TILES_IMG)
    bias = [jnp.where(column_tile < n, 0.0, neg_fill) for n in tiles]
    live = [(n > 0).astype(jnp.float32) for n in tiles]

    def front(b, first):
        query = stacked(query_ref, b * BLOCK, first, per_chunk)
        grad = stacked(grad_ref, b * BLOCK, first, per_chunk)
        scores = dot(query, keys_ref[slots[b]], NT) + bias[b]
        prob_grad = dot(grad, values_ref[slots[b]], NT)
        return query, grad, scores, prob_grad

    def middle(b, first, query, grad, scores, prob_grad):
        row_max = jnp.max(scores, axis=1, keepdims=True)
        terms = jnp.exp((scores - row_max) * score_scale)
        inverse_sum = live[b] / jnp.sum(terms, axis=1, keepdims=True)
        weights = terms * inverse_sum
        probs = weights.astype(jnp.bfloat16)
        out = dot(probs, values_ref[slots[b]], NN).astype(jnp.bfloat16)
        unstack(out_ref, b * BLOCK, first, per_chunk, out)
        delta = jnp.sum(grad.astype(jnp.float32) * out.astype(jnp.float32), axis=1, keepdims=True)
        dscore = (weights * (prob_grad - delta)).astype(jnp.bfloat16)
        return probs, dscore

    def back(b, first, query, grad, probs, dscore):
        query_grad = (dot(dscore, keys_ref[slots[b]], NN) * score_scale).astype(jnp.bfloat16)
        unstack(query_grad_ref, b * BLOCK, first, per_chunk, query_grad)
        value_term = dot(probs, grad, TN)
        key_term = dot(dscore, query, TN)
        if b == 0 and first == 0:
            value_acc[0] = value_term
            key_acc[0] = key_term
        else:
            value_acc[slots[b]] += value_term
            key_acc[slots[b]] += key_term

    def store_terms(slot, image):
        rows = image_slice(image)
        terms_ref[:, rows, :HD] = (
            (key_acc[slot] * score_scale).astype(jnp.bfloat16).reshape(groups, image_rows, HD)
        )
        terms_ref[:, rows, HD:] = value_acc[slot].astype(jnp.bfloat16).reshape(groups, image_rows, HD)

    load_image(0, images[0])

    @pl.when(mixed)
    def _():
        load_image(1, images[1])
        value_acc[1] = jnp.zeros((span, HD), jnp.float32)
        key_acc[1] = jnp.zeros((span, HD), jnp.float32)

    chunks = [(b, first) for b in range(2) for first in range(0, heads, per_chunk)]
    held = None
    for chunk in chunks:
        query, grad, scores, prob_grad = front(*chunk)
        if held is not None:
            back(*held)
        probs, dscore = middle(*chunk, query, grad, scores, prob_grad)
        held = (*chunk, query, grad, probs, dscore)
    back(*held)
    store_terms(0, images[0])

    @pl.when(mixed)
    def _():
        store_terms(1, images[1])

    @pl.when(jnp.logical_not(mixed))
    def _():
        terms_ref[:, image_slice(1 - images[0]), :] = jnp.zeros((groups, image_rows, 2 * HD), jnp.bfloat16)


def attention(info, query, out_grad, kv):
    groups, group_rows, _ = kv.shape
    span = groups * group_rows // 2
    vmem = pl.BlockSpec(memory_space=pltpu.VMEM)
    work = 6 * 2 * query.size * span
    return pl.pallas_call(
        attention_kernel,
        out_shape=[
            jax.ShapeDtypeStruct(query.shape, jnp.bfloat16),
            jax.ShapeDtypeStruct(query.shape, jnp.bfloat16),
            jax.ShapeDtypeStruct(kv.shape, jnp.bfloat16),
        ],
        in_specs=[vmem, vmem, vmem, vmem],
        out_specs=[vmem, vmem, vmem],
        scratch_shapes=[
            pltpu.VMEM((2, span, HD), jnp.bfloat16),
            pltpu.VMEM((2, span, HD), jnp.bfloat16),
            pltpu.VMEM((2, span, HD), jnp.float32),
            pltpu.VMEM((2, span, HD), jnp.float32),
        ],
        compiler_params=pltpu.CompilerParams(vmem_limit_bytes=40 * 1024 * 1024),
        cost_estimate=pl.CostEstimate(flops=work, bytes_accessed=5 * 1024 * 1024, transcendentals=query.size * span // HD),
        name="attention",
    )(info, query, out_grad, kv)


def prepare_kernel(seq_index, image_ref, tiles_ref, gain_ref, kv_ref, copies_ref, info_ref, normed_ref, inverse_ref, kept_gain_ref):
    heads = normed_ref.shape[1] // HD
    gain, image, tiles = (gain_ref[...], image_ref[...].astype(jnp.float32), tiles_ref[...].astype(jnp.float32))
    lane = lax.broadcasted_iota(jnp.int32, info_ref.shape, 1)
    begin = seq_index() * 2

    def entry(row, index):
        return jnp.sum(jnp.where(lane == index, row, 0.0), axis=1, keepdims=True)

    info = jnp.where(
        lane == 0,
        entry(image, begin),
        jnp.where(
            lane == 1,
            entry(image, begin + 1),
            jnp.where(lane == 2, entry(tiles, begin), entry(tiles, begin + 1)),
        ),
    )
    info_ref[...] = info
    kept_gain_ref[...] = gain
    for t in range(heads):
        pre = kv_ref[:, 2 * t * HD : (2 * t + 1) * HD].astype(jnp.float32)
        values = kv_ref[:, (2 * t + 1) * HD : (2 * t + 2) * HD]
        inverse = lax.rsqrt(jnp.mean(pre * pre, axis=1, keepdims=True) + epsilon)
        normed = pre * inverse
        keys = (normed * gain).astype(jnp.bfloat16)
        normed_ref[:, t * HD : (t + 1) * HD] = normed
        inverse_ref[:, t * HD : (t + 1) * HD] = jnp.broadcast_to(inverse, normed.shape)
        for copy in range(t, copies_ref.shape[0], heads):
            copies_ref[copy, :, :HD] = keys
            copies_ref[copy, :, HD:] = values


def prepare(seq_index, span_image, span_tiles, key_gain, vision_kv, copies):
    rows, columns = vision_kv.shape
    heads = columns // (2 * HD)
    vmem = pl.BlockSpec(memory_space=pltpu.VMEM)
    return pl.pallas_call(
        functools.partial(prepare_kernel, seq_index),
        out_shape=[
            jax.ShapeDtypeStruct((copies * heads, rows, 2 * HD), jnp.bfloat16),
            jax.ShapeDtypeStruct((1, HD), jnp.float32),
            jax.ShapeDtypeStruct((rows, heads * HD), jnp.float32),
            jax.ShapeDtypeStruct((rows, heads * HD), jnp.float32),
            jax.ShapeDtypeStruct((1, HD), jnp.float32),
        ],
        in_specs=[vmem] * 4,
        out_specs=[vmem] * 5,
        compiler_params=pltpu.CompilerParams(vmem_limit_bytes=8 * 1024 * 1024),
        name="prepare",
    )(span_image.reshape(1, -1), span_tiles.reshape(1, -1), key_gain.reshape(1, -1), vision_kv)


def finish_kernel(got_ref, normed_ref, inverse_ref, gain_ref, out_ref):
    heads = out_ref.shape[1] // (2 * HD)
    gain = gain_ref[...]
    for t in range(heads):
        key_grad, value_grad = (
            sum(got_ref[k, :, part * HD : (part + 1) * HD].astype(jnp.float32) for k in range(t, got_ref.shape[0], heads))
            for part in range(2)
        )
        normed = normed_ref[:, t * HD : (t + 1) * HD]
        inverse = inverse_ref[:, t * HD : (t + 1) * HD]
        scaled = key_grad * gain
        pre_grad = inverse * (scaled - normed * jnp.mean(scaled * normed, axis=1, keepdims=True))
        out_ref[:, 2 * t * HD : (2 * t + 1) * HD] = pre_grad.astype(jnp.bfloat16)
        out_ref[:, (2 * t + 1) * HD : (2 * t + 2) * HD] = value_grad.astype(jnp.bfloat16)


def finish(got, normed, inverse, gain):
    rows = normed.shape[0]
    vmem = pl.BlockSpec(memory_space=pltpu.VMEM)
    return pl.pallas_call(
        finish_kernel,
        out_shape=jax.ShapeDtypeStruct((rows, 2 * normed.shape[1]), jnp.bfloat16),
        in_specs=[vmem] * 4,
        out_specs=vmem,
        compiler_params=pltpu.CompilerParams(vmem_limit_bytes=8 * 1024 * 1024),
        name="finish",
    )(got, normed, inverse, gain)


def spread(rows, axes, copies):
    return lax.all_to_all(
        lax.optimization_barrier(jnp.broadcast_to(rows, (copies,) + rows.shape)), axes, split_axis=0, concat_axis=0
    )


def fold(terms, axis, parts):
    got = lax.all_to_all(terms.reshape((parts, -1) + terms.shape[1:]), axis, split_axis=0, concat_axis=0)
    return jnp.sum(got.astype(jnp.float32), axis=0).astype(jnp.bfloat16)


def body(query, vision_kv, key_gain, out_grad, span_image, span_tiles):
    z, x, cores, tp = (lax.axis_size(name) for name in ("z", "x", "c", "tp"))
    own_rows = vision_kv.shape[0]

    def seq_index():
        return (lax.axis_index("z") * x + lax.axis_index("x")) * cores + lax.axis_index("c")

    copies, info, normed, inverse, gain = prepare(
        seq_index, span_image, span_tiles, key_gain, vision_kv, z
    )
    along_z = lax.all_to_all(copies, ("z", "tp"), split_axis=0, concat_axis=0, tiled=True)
    column = along_z.reshape(z * tp * own_rows, 2 * HD)
    plane = spread(column, "x", x)
    kv = spread(plane, "c", cores).reshape(cores * x, z * tp * own_rows, 2 * HD)

    attn_out, query_grad, terms = attention(info, query, out_grad, kv)

    terms = fold(terms, "c", cores)
    terms = fold(terms, "x", x)
    got = lax.all_to_all(
        terms.reshape(z * tp, own_rows, 2 * HD), ("z", "tp"), split_axis=0, concat_axis=0, tiled=True
    )
    return (attn_out, query_grad, finish(got, normed, inverse, gain))


def solution(mesh):
    fine = Mesh(mesh.devices.reshape(8, 4, 2, 8), ("z", "x", "c", "tp"))
    seq = ("z", "x", "c")
    in_specs = (P(seq, "tp"), P(seq + ("tp",), None), P(), P(seq, "tp"), P(), P())
    out_specs = (P(seq, "tp"), P(seq, "tp"), P(seq + ("tp",), None))
    return jax.shard_map(body, mesh=fine, in_specs=in_specs, out_specs=out_specs, check_vma=False)
```

time: 91.1 us -> 88.4 us (0.970)
  blocking collectives: 63.3 us -> 78.7 us
  waiting for transfers between devices: 11.5 us -> 0 us
  starting transfers between devices: 4.62 us -> 0 us
  local copies, waits for them, and re-layouts: 3.06 us -> 1.57 us
    all_to_all x1 -> x2, blocking collectives: 28.5 us -> 43.9 us  [the longest x1 28.5 us: body(): lax.all_to_all(copies, ('z', 'tp'), split_axis=0, concat_axis=0, tiled=True)]
    all_to_all x1 -> x0, waiting for transfers between devices: 11.5 us -> none  [body(): lax.all_to_all(terms.reshape(z * tp, own_rows, 2 * HD), ('z', 'tp'), spli...]
    all_to_all x1 -> x0, starting transfers between devices: 4.62 us -> none  [body(): lax.all_to_all(terms.reshape(z * tp, own_rows, 2 * HD), ('z', 'tp'), spli...]
    unnamed x13 -> x12, local copies, waits for them, and re-layouts: 2.03 us -> 1.39 us
    pallas_call x1 -> x3, Pallas kernels: 6.41 us -> 6.38 us  [the longest x1 5.56 us: attention(): pl.pallas_call(attention_kernel, out_shape=[jax.ShapeDtypeStruct(query.sh...]
  transfers between devices with their start and end apart: 1 -> 0, of which waited for: 1 -> 0; matrix products, arithmetic and copies ran while one was open for 0% -> 0% of each run, Pallas kernels for 0% -> 0%
where the time goes in v2:
time: 88.4 us; the launch traced here: 88 us
  blocking collectives  78.7 us (89%)
  Pallas kernels  6.38 us (7%)
  local copies, waits for them, and re-layouts  1.57 us (2%)
    all_to_all x1, blocking collectives, body(): lax.all_to_all(copies, ('z', 'tp'), split_axis=0, concat_axis=0, tiled=True)  28.5 us
    all_to_all x2, blocking collectives, spread(): lax.all_to_all(lax.optimization_barrier(jnp.broadcast_to(rows, (copies,)...  18.6 us
    all_to_all x2, blocking collectives, fold(): lax.all_to_all(terms.reshape((parts, -1) + terms.shape[1:]), axis, split_...  16.2 us
    all_to_all x1, blocking collectives, body(): lax.all_to_all(terms.reshape(z * tp, own_rows, 2 * HD), ('z', 'tp'), spli...  15.4 us
    pallas_call x1, Pallas kernels, attention(): pl.pallas_call(attention_kernel, out_shape=[jax.ShapeDtypeStruct(query.sh...  5.56 us

profile of v2, /device:TPU:1, one launch (start us, length us, event | category | flops | bytes accessed | tf_op | source)
XLA Modules:
  0.0 88.0 jit_solution(8637509491746692059)
XLA Ops:
  0.6 0.0 copy-start.1
  0.6 0.0 copy-start.2
  0.7 0.0 copy-start.3
  0.7 0.6 copy-done.1
  1.3 0.0 copy-done.2
  1.3 0.0 copy-done.3
  1.3 0.0 copy-start
  1.3 0.7 copy-done
  2.0 0.1 prepare.1
  2.2 28.5 %all_to_all.30 = bf16[64,4,256]{2,1,0:T(4,128)(2,1)S(1)} all-to-all(bf16[64,4,256]{2,1,0:T(4,128)(2,1)S(1)} %get-tuple-element.12), channel_id=1, replica_groups=mesh['z'=8,'x'=4,'c'=2,'tp'=8] {'z','tp'}, dimensions={0} | all-to-all | bytes 262144 | tf_op jit(solution)/shard_map/all_to_all | solution.py:261
  30.7 10.8 %all_to_all.31 = bf16[4,256,256]{2,1,0:T(8,128)(2,1)S(1)} all-to-all(bf16[4,256,256]{2,1,0:T(8,128)(2,1)S(1)} %broadcast_in_dim.6), channel_id=1, replica_groups=mesh['z'=8,'x'=4,'c'=2,'tp'=8] {'x'}, dimensions={0} | all-to-all | bytes 1048576 | tf_op jit(solution)/shard_map/all_to_all | solution.py:241
  41.5 0.1 broadcast_in_dim.7
  41.6 0.0 copy-start.4
  41.6 0.0 copy-start.5
  41.6 7.9 %all_to_all.32 = bf16[2,4,256,256]{3,2,1,0:T(8,128)(2,1)S(1)} all-to-all(bf16[2,4,256,256]{3,2,1,0:T(8,128)(2,1)S(1)} %broadcast_in_dim.7), channel_id=1, replica_groups=mesh['z'=8,'x'=4,'c'=2,'tp'=8] {'c'}, dimensions={0} | all-to-all | bytes 2097152 | tf_op jit(solution)/shard_map/all_to_all | solution.py:241
  49.5 0.0 copy-done.4
  49.5 0.0 copy-done.5
  49.5 5.6 %attention.1 = (bf16[128,1024]{1,0:T(8,128)(2,1)}, bf16[128,1024]{1,0:T(8,128)(2,1)}, bf16[8,256,256]{2,1,0:T(8,128)(2,1)S(1)}) custom-call(f32[1,128]{1,0:T(1,128)S(1)} %get-tuple-element.11.info_ref, bf16[128,1024]{1,0:T(8,128)(2,1)S(1)} %copy-done.4, bf16[128,1024]{1,0:T(8,128)(2,1)S(1)} %copy-done.5, bf16[8,256,256]{2,1,0:T(8,128)(2,1)S(1)} %bitcast.6), custom_call_target="tpu_custom_call" | custom-call | flops 1610612736 | bytes 5242880 | tf_op jit(solution)/shard_map/attention/pallas_call | solution.py:137
  55.0 4.6 %all_to_all.33 = bf16[2,4,256,256]{3,2,1,0:T(8,128)(2,1)S(1)} all-to-all(bf16[2,4,256,256]{3,2,1,0:T(8,128)(2,1)S(1)} %bitcast.7), channel_id=1, replica_groups=mesh['z'=8,'x'=4,'c'=2,'tp'=8] {'c'}, dimensions={0} | all-to-all | bytes 2097152 | tf_op jit(solution)/shard_map/all_to_all | solution.py:247
  59.6 0.5 reduce_sum.24
  60.0 11.6 %all_to_all.34 = bf16[4,1,256,256]{3,2,1,0:T(8,128)(2,1)S(1)} all-to-all(bf16[4,1,256,256]{3,2,1,0:T(8,128)(2,1)S(1)} %bitcast.11), channel_id=1, replica_groups=mesh['z'=8,'x'=4,'c'=2,'tp'=8] {'x'}, dimensions={0} | all-to-all | bytes 1048576 | tf_op jit(solution)/shard_map/all_to_all | solution.py:247
  71.7 0.1 reduce_sum.25
  71.8 15.4 %all_to_all.35.got_ref = bf16[64,4,256]{2,1,0:T(4,128)(2,1)S(1)} all-to-all(bf16[64,4,256]{2,1,0:T(4,128)(2,1)S(1)} %reshape.39), channel_id=1, replica_groups=mesh['z'=8,'x'=4,'c'=2,'tp'=8] {'z','tp'}, dimensions={0} | all-to-all | bytes 262144 | tf_op jit(solution)/shard_map/all_to_all | solution.py:270
  87.2 0.7 finish.1
  (3 shorter events, 0.1 us)
Async XLA Ops:
  0.6 0.7 copy-start.1
  0.6 0.7 copy-start.2
  0.7 0.7 copy-start.3
  1.3 0.7 copy-start
  41.6 7.9 %copy-start.4 = (bf16[128,1024]{1,0:T(8,128)(2,1)S(1)}, bf16[128,1024]{1,0:T(8,128)(2,1)}, u32[]{:S(2)}) copy-start(bf16[128,1024]{1,0:T(8,128)(2,1)} %query_ref.1) | copy-start | bytes 786436
  41.6 7.9 %copy-start.5 = (bf16[128,1024]{1,0:T(8,128)(2,1)S(1)}, bf16[128,1024]{1,0:T(8,128)(2,1)}, u32[]{:S(2)}) copy-start(bf16[128,1024]{1,0:T(8,128)(2,1)} %grad_ref.1) | copy-start | bytes 786436

commit v3 on v2

--- a/solution.py
+++ b/solution.py
@@ -26,27 +26,39 @@
 
 
 def attention_kernel(
-    info_ref, query_ref, grad_ref, kv_ref, out_ref, query_grad_ref, terms_ref, keys_ref, values_ref, key_acc, value_acc,
+    image_rows, info_ref, query_ref, grad_ref, kv_ref, out_ref, query_grad_ref, terms_ref,
+    key_acc, value_acc, keys_ref, values_ref,
 ):
     groups, group_rows, _ = kv_ref.shape
-    image_rows = group_rows // 2
+    both = group_rows != image_rows
     part = image_rows // TILES_IMG
     span = groups * image_rows
     heads = query_ref.shape[1] // HD
     lane = lax.broadcasted_iota(jnp.int32, info_ref.shape, 1)
-    images, tiles = (
-        [jnp.sum(jnp.where(lane == k, info_ref[...], 0.0)).astype(jnp.int32) for k in pair] for pair in ((0, 1), (2, 3))
-    )
-    mixed = images[0] != images[1]
-    slots = [0, mixed.astype(jnp.int32)]
+    tiles = [jnp.sum(jnp.where(lane == k, info_ref[...], 0.0)).astype(jnp.int32) for k in (2, 3)]
+    slots = [0, 0]
+    images = [0, 0]
+    if both:
+        images = [jnp.sum(jnp.where(lane == k, info_ref[...], 0.0)).astype(jnp.int32) for k in range(2)]
+        mixed = images[0] != images[1]
+        slots = [0, mixed.astype(jnp.int32)]
 
     def image_slice(image):
-        return pl.ds(pl.multiple_of(image * image_rows, image_rows), image_rows)
+        return pl.ds(pl.multiple_of(image * image_rows, image_rows), image_rows) if both else slice(None)
+
+    def view(ref, slot):
+        return ref.at[slot] if both else ref
 
     def load_image(slot, image):
         rows = image_slice(image)
-        keys_ref[slot] = kv_ref[:, rows, :HD].reshape(span, HD)
-        values_ref[slot] = kv_ref[:, rows, HD:].reshape(span, HD)
+        view(keys_ref, slot)[...] = kv_ref[:, rows, :HD].reshape(span, HD)
+        view(values_ref, slot)[...] = kv_ref[:, rows, HD:].reshape(span, HD)
+
+    def keys_of(b):
+        return keys_ref[slots[b]] if both else kv_ref[:, :, :HD].reshape(span, HD)
+
+    def values_of(b):
+        return values_ref[slots[b]] if both else kv_ref[:, :, HD:].reshape(span, HD)
 
     def stacked(ref, row, first, count):
         return jnp.concatenate(
@@ -59,15 +71,14 @@
 
     per_chunk = 4
     column = lax.broadcasted_iota(jnp.int32, (1, span), 1)
-    column_tile = lax.rem(lax.div(column, part), TILES_IMG)
-    bias = [jnp.where(column_tile < n, 0.0, neg_fill) for n in tiles]
+    bias = [jnp.where((column & (image_rows - 1)) < n * part, 0.0, neg_fill) for n in tiles]
     live = [(n > 0).astype(jnp.float32) for n in tiles]
 
     def front(b, first):
         query = stacked(query_ref, b * BLOCK, first, per_chunk)
         grad = stacked(grad_ref, b * BLOCK, first, per_chunk)
-        scores = dot(query, keys_ref[slots[b]], NT) + bias[b]
-        prob_grad = dot(grad, values_ref[slots[b]], NT)
+        scores = dot(query, keys_of(b), NT) + bias[b]
+        prob_grad = dot(grad, values_of(b), NT)
         return query, grad, scores, prob_grad
 
     def middle(b, first, query, grad, scores, prob_grad):
@@ -76,38 +87,39 @@
         inverse_sum = live[b] / jnp.sum(terms, axis=1, keepdims=True)
         weights = terms * inverse_sum
         probs = weights.astype(jnp.bfloat16)
-        out = dot(probs, values_ref[slots[b]], NN).astype(jnp.bfloat16)
+        out = dot(probs, values_of(b), NN).astype(jnp.bfloat16)
         unstack(out_ref, b * BLOCK, first, per_chunk, out)
         delta = jnp.sum(grad.astype(jnp.float32) * out.astype(jnp.float32), axis=1, keepdims=True)
         dscore = (weights * (prob_grad - delta)).astype(jnp.bfloat16)
         return probs, dscore
 
     def back(b, first, query, grad, probs, dscore):
-        query_grad = (dot(dscore, keys_ref[slots[b]], NN) * score_scale).astype(jnp.bfloat16)
+        query_grad = (dot(dscore, keys_of(b), NN) * score_scale).astype(jnp.bfloat16)
         unstack(query_grad_ref, b * BLOCK, first, per_chunk, query_grad)
         value_term = dot(probs, grad, TN)
         key_term = dot(dscore, query, TN)
         if b == 0 and first == 0:
-            value_acc[0] = value_term
-            key_acc[0] = key_term
+            view(value_acc, 0)[...] = value_term
+            view(key_acc, 0)[...] = key_term
         else:
-            value_acc[slots[b]] += value_term
-            key_acc[slots[b]] += key_term
+            view(value_acc, slots[b])[...] += value_term
+            view(key_acc, slots[b])[...] += key_term
 
     def store_terms(slot, image):
         rows = image_slice(image)
         terms_ref[:, rows, :HD] = (
-            (key_acc[slot] * score_scale).astype(jnp.bfloat16).reshape(groups, image_rows, HD)
+            (view(key_acc, slot)[...] * score_scale).astype(jnp.bfloat16).reshape(groups, image_rows, HD)
         )
-        terms_ref[:, rows, HD:] = value_acc[slot].astype(jnp.bfloat16).reshape(groups, image_rows, HD)
-
-    load_image(0, images[0])
-
-    @pl.when(mixed)
-    def _():
-        load_image(1, images[1])
-        value_acc[1] = jnp.zeros((span, HD), jnp.float32)
-        key_acc[1] = jnp.zeros((span, HD), jnp.float32)
+        terms_ref[:, rows, HD:] = view(value_acc, slot)[...].astype(jnp.bfloat16).reshape(groups, image_rows, HD)
+
+    if both:
+        load_image(0, images[0])
+
+        @pl.when(mixed)
+        def _():
+            load_image(1, images[1])
+            value_acc[1] = jnp.zeros((span, HD), jnp.float32)
+            key_acc[1] = jnp.zeros((span, HD), jnp.float32)
 
     chunks = [(b, first) for b in range(2) for first in range(0, heads, per_chunk)]
     held = None
@@ -120,22 +132,26 @@
     back(*held)
     store_terms(0, images[0])
 
-    @pl.when(mixed)
-    def _():
-        store_terms(1, images[1])
-
-    @pl.when(jnp.logical_not(mixed))
-    def _():
-        terms_ref[:, image_slice(1 - images[0]), :] = jnp.zeros((groups, image_rows, 2 * HD), jnp.bfloat16)
-
-
-def attention(info, query, out_grad, kv):
-    groups, group_rows, _ = kv.shape
-    span = groups * group_rows // 2
+    if both:
+
+        @pl.when(mixed)
+        def _():
+            store_terms(1, images[1])
+
+        @pl.when(jnp.logical_not(mixed))
+        def _():
+            terms_ref[:, image_slice(1 - images[0]), :] = jnp.zeros((groups, image_rows, 2 * HD), jnp.bfloat16)
+
+
+def attention(info, query, out_grad, kv, image_rows):
+    span = kv.shape[0] * image_rows
+    slots = kv.shape[1] // image_rows
+    held = (slots, span, HD) if slots > 1 else (span, HD)
+    scratch = [pltpu.VMEM(held, dtype) for dtype in (jnp.float32, jnp.float32, jnp.bfloat16, jnp.bfloat16)]
     vmem = pl.BlockSpec(memory_space=pltpu.VMEM)
     work = 6 * 2 * query.size * span
     return pl.pallas_call(
-        attention_kernel,
+        functools.partial(attention_kernel, image_rows),
         out_shape=[
             jax.ShapeDtypeStruct(query.shape, jnp.bfloat16),
             jax.ShapeDtypeStruct(query.shape, jnp.bfloat16),
@@ -143,23 +159,22 @@
         ],
         in_specs=[vmem, vmem, vmem, vmem],
         out_specs=[vmem, vmem, vmem],
-        scratch_shapes=[
-            pltpu.VMEM((2, span, HD), jnp.bfloat16),
-            pltpu.VMEM((2, span, HD), jnp.bfloat16),
-            pltpu.VMEM((2, span, HD), jnp.float32),
-            pltpu.VMEM((2, span, HD), jnp.float32),
-        ],
+        scratch_shapes=scratch,
         compiler_params=pltpu.CompilerParams(vmem_limit_bytes=40 * 1024 * 1024),
         cost_estimate=pl.CostEstimate(flops=work, bytes_accessed=5 * 1024 * 1024, transcendentals=query.size * span // HD),
         name="attention",
     )(info, query, out_grad, kv)
 
 
-def prepare_kernel(seq_index, image_ref, tiles_ref, gain_ref, kv_ref, copies_ref, info_ref, normed_ref, inverse_ref, kept_gain_ref):
+def prepare_kernel(
+    mesh_index, image_ref, tiles_ref, gain_ref, kv_ref,
+    copies_ref, info_ref, plane_ref, normed_ref, inverse_ref, kept_gain_ref,
+):
     heads = normed_ref.shape[1] // HD
     gain, image, tiles = (gain_ref[...], image_ref[...].astype(jnp.float32), tiles_ref[...].astype(jnp.float32))
     lane = lax.broadcasted_iota(jnp.int32, info_ref.shape, 1)
-    begin = seq_index() * 2
+    plane, place, cores = mesh_index()
+    begin = (plane + place) * 2
 
     def entry(row, index):
         return jnp.sum(jnp.where(lane == index, row, 0.0), axis=1, keepdims=True)
@@ -173,7 +188,17 @@
             jnp.where(lane == 2, entry(tiles, begin), entry(tiles, begin + 1)),
         ),
     )
+    mixed = jnp.sum(jnp.where((lane & 1) == 1, image, -image), axis=1, keepdims=True)
     info_ref[...] = info
+    members = plane_ref.shape[0]
+    member = lax.broadcasted_iota(jnp.int32, (members, HD), 0)
+    member_lane = lax.broadcasted_iota(jnp.int32, (members, HD), 1)
+    first = plane * 2
+    for core in range(cores):
+        place = member - core * (members // cores)
+        first = first + jnp.where((place >= 0) & (place < members // cores), (place * cores + core) * 2, 0)
+    seen = jnp.sum(jnp.where(member_lane == first, image, 0.0), axis=1, keepdims=True)
+    plane_ref[...] = jnp.broadcast_to(seen, plane_ref.shape)
     kept_gain_ref[...] = gain
     for t in range(heads):
         pre = kv_ref[:, 2 * t * HD : (2 * t + 1) * HD].astype(jnp.float32)
@@ -188,21 +213,22 @@
             copies_ref[copy, :, HD:] = values
 
 
-def prepare(seq_index, span_image, span_tiles, key_gain, vision_kv, copies):
+def prepare(mesh_index, members, span_image, span_tiles, key_gain, vision_kv, copies):
     rows, columns = vision_kv.shape
     heads = columns // (2 * HD)
     vmem = pl.BlockSpec(memory_space=pltpu.VMEM)
     return pl.pallas_call(
-        functools.partial(prepare_kernel, seq_index),
+        functools.partial(prepare_kernel, mesh_index),
         out_shape=[
             jax.ShapeDtypeStruct((copies * heads, rows, 2 * HD), jnp.bfloat16),
             jax.ShapeDtypeStruct((1, HD), jnp.float32),
+            jax.ShapeDtypeStruct((members, 2 * HD), jnp.float32),
             jax.ShapeDtypeStruct((rows, heads * HD), jnp.float32),
             jax.ShapeDtypeStruct((rows, heads * HD), jnp.float32),
             jax.ShapeDtypeStruct((1, HD), jnp.float32),
         ],
         in_specs=[vmem] * 4,
-        out_specs=[vmem] * 5,
+        out_specs=[vmem] * 6,
         compiler_params=pltpu.CompilerParams(vmem_limit_bytes=8 * 1024 * 1024),
         name="prepare",
     )(span_image.reshape(1, -1), span_tiles.reshape(1, -1), key_gain.reshape(1, -1), vision_kv)
@@ -237,6 +263,37 @@
     )(got, normed, inverse, gain)
 
 
+def route_kernel(plane_ref, column_ref, out_ref):
+    members, image_rows, _ = out_ref.shape
+    first = column_ref[:image_rows, :]
+    second = column_ref[image_rows:, :]
+    for k in range(members):
+        out_ref[k] = jnp.where(plane_ref[k : k + 1, :] > 0.5, second, first)
+
+
+def collect_kernel(plane_ref, got_ref, out_ref):
+    members, image_rows, _ = got_ref.shape
+    totals = [0.0, 0.0]
+    for k in range(members):
+        term = got_ref[k].astype(jnp.float32)
+        second = plane_ref[k : k + 1, :] > 0.5
+        totals = [totals[0] + jnp.where(second, 0.0, term), totals[1] + jnp.where(second, term, 0.0)]
+    for image in range(2):
+        out_ref[image * image_rows : (image + 1) * image_rows, :] = totals[image].astype(jnp.bfloat16)
+
+
+def small_call(kernel, shape, *args):
+    vmem = pl.BlockSpec(memory_space=pltpu.VMEM)
+    return pl.pallas_call(
+        kernel,
+        out_shape=jax.ShapeDtypeStruct(shape, jnp.bfloat16),
+        in_specs=[vmem] * len(args),
+        out_specs=vmem,
+        compiler_params=pltpu.CompilerParams(vmem_limit_bytes=8 * 1024 * 1024),
+        name=kernel.__name__,
+    )(*args)
+
+
 def spread(rows, axes, copies):
     return lax.all_to_all(
         lax.optimization_barrier(jnp.broadcast_to(rows, (copies,) + rows.shape)), axes, split_axis=0, concat_axis=0
@@ -251,22 +308,36 @@
 def body(query, vision_kv, key_gain, out_grad, span_image, span_tiles):
     z, x, cores, tp = (lax.axis_size(name) for name in ("z", "x", "c", "tp"))
     own_rows = vision_kv.shape[0]
-
-    def seq_index():
-        return (lax.axis_index("z") * x + lax.axis_index("x")) * cores + lax.axis_index("c")
-
-    copies, info, normed, inverse, gain = prepare(
-        seq_index, span_image, span_tiles, key_gain, vision_kv, z
+    column_rows = z * tp * own_rows
+    image_rows = column_rows // 2
+    members = x * cores
+
+    def mesh_index():
+        return lax.axis_index("z") * members, lax.axis_index("x") * cores + lax.axis_index("c"), cores
+
+    mixed = jnp.sum(jnp.where(jnp.arange(span_image.shape[0]) % 2 == 1, span_image, -span_image)) > 0
+
+    copies, info, plane, normed, inverse, gain = prepare(
+        mesh_index, members, span_image, span_tiles, key_gain, vision_kv, z
     )
     along_z = lax.all_to_all(copies, ("z", "tp"), split_axis=0, concat_axis=0, tiled=True)
-    column = along_z.reshape(z * tp * own_rows, 2 * HD)
-    plane = spread(column, "x", x)
-    kv = spread(plane, "c", cores).reshape(cores * x, z * tp * own_rows, 2 * HD)
-
-    attn_out, query_grad, terms = attention(info, query, out_grad, kv)
-
-    terms = fold(terms, "c", cores)
-    terms = fold(terms, "x", x)
+    column = along_z.reshape(column_rows, 2 * HD)
+
+    def one_image(info, plane, column, query, out_grad):
+        routed = small_call(route_kernel, (members, image_rows, 2 * HD), plane, column)
+        kv = lax.all_to_all(routed, ("c", "x"), split_axis=0, concat_axis=0, tiled=True)
+        attn_out, query_grad, terms = attention(info, query, out_grad, kv, image_rows)
+        got = lax.all_to_all(terms, ("c", "x"), split_axis=0, concat_axis=0, tiled=True)
+        return attn_out, query_grad, small_call(collect_kernel, column.shape, plane, got)
+
+    def two_images(info, plane, column, query, out_grad):
+        kv = spread(spread(column, "x", x), "c", cores).reshape(members, column_rows, 2 * HD)
+        attn_out, query_grad, terms = attention(info, query, out_grad, kv, image_rows)
+        return attn_out, query_grad, fold(fold(terms, "c", cores), "x", x).reshape(column.shape)
+
+    attn_out, query_grad, terms = lax.cond(
+        mixed, two_images, one_image, info, plane, column, query, out_grad
+    )
     got = lax.all_to_all(
         terms.reshape(z * tp, own_rows, 2 * HD), ("z", "tp"), split_axis=0, concat_axis=0, tiled=True
     )

time: 88.4 us -> 89.3 us (1.010)
  blocking collectives: 78.7 us -> 50.1 us
  starting transfers between devices: 0 us -> 17.3 us
  waiting for transfers between devices: 0 us -> 10.3 us
    all_to_all x1 -> x0, blocking collectives: 28.5 us -> none  [body(): lax.all_to_all(copies, ('z', 'tp'), split_axis=0, concat_axis=0, tiled=True)]
    all_to_all x0 -> x1, starting transfers between devices: none -> 17.3 us  [body(): lax.all_to_all(copies, ('z', 'tp'), split_axis=0, concat_axis=0, tiled=True)]
    all_to_all x0 -> x1, waiting for transfers between devices: none -> 10.3 us  [body(): lax.all_to_all(copies, ('z', 'tp'), split_axis=0, concat_axis=0, tiled=True)]
  transfers between devices with their start and end apart: 0 -> 1, of which waited for: 0 -> 1; matrix products, arithmetic and copies ran while one was open for 0% -> 1% of each run, Pallas kernels for 0% -> 0%
where the time goes in v3:
time: 89.3 us; the launch traced here: 88.8 us
  blocking collectives  50.1 us (56%)
  starting transfers between devices  17.3 us (19%)
  waiting for transfers between devices  10.3 us (12%)
  Pallas kernels  7.04 us (8%)
  local copies, waits for them, and re-layouts  1.56 us (2%)
  between operations  1.34 us (2%)
  other arithmetic  1.18 us (1%)
    all_to_all x2, blocking collectives, spread(): lax.all_to_all(lax.optimization_barrier(jnp.broadcast_to(rows, (copies,)...  18.5 us
    all_to_all x1, starting transfers between devices, body(): lax.all_to_all(copies, ('z', 'tp'), split_axis=0, concat_axis=0, tiled=True)  17.3 us
    all_to_all x2, blocking collectives, fold(): lax.all_to_all(terms.reshape((parts, -1) + terms.shape[1:]), axis, split_...  16.2 us
    all_to_all x1, blocking collectives, body(): lax.all_to_all(terms.reshape(z * tp, own_rows, 2 * HD), ('z', 'tp'), spli...  15.4 us
    all_to_all x1, waiting for transfers between devices, body(): lax.all_to_all(copies, ('z', 'tp'), split_axis=0, concat_axis=0, tiled=True)  10.3 us
    pallas_call x1, Pallas kernels, attention(): pl.pallas_call(functools.partial(attention_kernel, image_rows), out_shape...  5.56 us
  transfers between devices with their start and end apart: 1, of which 1 were waited for; matrix products, arithmetic and copies ran while one was open for 1% of the time, Pallas kernels for 0%

profile of v3, /device:TPU:1, one launch (start us, length us, event | category | flops | bytes accessed | tf_op | source)
XLA Modules:
  0.0 88.8 jit_solution(3252590774670747508)
XLA Ops:
  0.6 0.0 copy-start.1
  0.6 0.0 copy-start.2
  0.7 0.0 copy-start.3
  0.7 0.6 copy-done.1
  1.3 0.0 copy-done.2
  1.3 0.0 copy-done.3
  1.3 0.0 copy-start
  1.3 0.7 copy-done
  2.0 0.8 prepare.1
  2.8 0.0 copy-start.4
  2.8 0.0 copy-start.5
  2.8 17.3 %all-to-all-start.6 = ((bf16[64,4,256]{2,1,0:T(4,128)(2,1)}), bf16[64,4,256]{2,1,0:T(4,128)(2,1)S(1)}, u32[]{:S(2)}, u32[]{:S(2)}) async-start(bf16[64,4,256]{2,1,0:T(4,128)(2,1)} %get-tuple-element.46), calls=%async_computation.6 | async-start | bytes 262144 | tf_op jit(solution)/shard_map/all_to_all | solution.py:323
  20.1 0.6 fusion
  21.4 10.3 %all-to-all-done.6 = bf16[64,4,256]{2,1,0:T(4,128)(2,1)S(1)} async-done(((bf16[64,4,256]{2,1,0:T(4,128)(2,1)}), bf16[64,4,256]{2,1,0:T(4,128)(2,1)S(1)}, u32[]{:S(2)}, u32[]{:S(2)}) %all-to-all-start.6) | async-done | bytes 131104 | tf_op jit(solution)/shard_map/all_to_all | solution.py:323
  31.7 0.0 copy-done.4
  31.7 0.0 copy-done.5
  31.7 41.0 %conditional.1 = (bf16[128,1024]{1,0:T(8,128)(2,1)}, bf16[128,1024]{1,0:T(8,128)(2,1)}, bf16[256,256]{1,0:T(8,128)(2,1)S(1)}) conditional(s32[]{:T(128)} %convert_element_type.2, (f32[8,256]{1,0:T(8,128)S(1)}, bf16[256,256]{1,0:T(8,128)(2,1)S(1)}, f32[1,128]{1,0:T(1,128)S(1)}, bf16[128,1024]{1,0:T(8,128)(2,1)S(1)}, ...), branch_computations={%region_1.2_spmd, %region_2.5_spmd} | conditional | flops 1611071488 | bytes 15990812 | solution.py:338
  31.7 10.8 %all_to_all.36 = bf16[4,256,256]{2,1,0:T(8,128)(2,1)S(1)} all-to-all(bf16[4,256,256]{2,1,0:T(8,128)(2,1)S(1)} %broadcast_in_dim.4), channel_id=1, replica_groups=mesh['z'=8,'x'=4,'c'=2,'tp'=8] {'x'}, dimensions={0} | all-to-all | bytes 1048576 | tf_op jit(solution)/shard_map/cond/branch_1_fun/all_to_all | solution.py:298
  42.5 0.1 broadcast_in_dim.5
  42.6 7.7 %all_to_all.37 = bf16[2,4,256,256]{3,2,1,0:T(8,128)(2,1)S(1)} all-to-all(bf16[2,4,256,256]{3,2,1,0:T(8,128)(2,1)S(1)} %broadcast_in_dim.5), channel_id=1, replica_groups=mesh['z'=8,'x'=4,'c'=2,'tp'=8] {'c'}, dimensions={0} | all-to-all | bytes 2097152 | tf_op jit(solution)/shard_map/cond/branch_1_fun/all_to_all | solution.py:298
  50.3 5.6 %attention.3 = (bf16[128,1024]{1,0:T(8,128)(2,1)}, bf16[128,1024]{1,0:T(8,128)(2,1)}, bf16[8,256,256]{2,1,0:T(8,128)(2,1)S(1)}) custom-call(f32[1,128]{1,0:T(1,128)S(1)} %get-tuple-element.26.info_ref, bf16[128,1024]{1,0:T(8,128)(2,1)S(1)} %get-tuple-element.27.query_ref, bf16[128,1024]{1,0:T(8,128)(2,1)S(1)} %get-tuple-element.28.grad_ref, ...), custom_call_target="tpu_custom_call" | custom-call | flops 1610612736 | bytes 5242880 | tf_op jit(solution)/shard_map/cond/branch_1_fun/attention/pallas_call | solution.py:153
  55.9 4.6 %all_to_all.38 = bf16[2,4,256,256]{3,2,1,0:T(8,128)(2,1)S(1)} all-to-all(bf16[2,4,256,256]{3,2,1,0:T(8,128)(2,1)S(1)} %bitcast.7), channel_id=1, replica_groups=mesh['z'=8,'x'=4,'c'=2,'tp'=8] {'c'}, dimensions={0} | all-to-all | bytes 2097152 | tf_op jit(solution)/shard_map/cond/branch_1_fun/all_to_all | solution.py:304
  60.4 0.5 reduce_sum.30
  60.9 11.6 %all_to_all.39 = bf16[4,1,256,256]{3,2,1,0:T(8,128)(2,1)S(1)} all-to-all(bf16[4,1,256,256]{3,2,1,0:T(8,128)(2,1)S(1)} %bitcast.11), channel_id=1, replica_groups=mesh['z'=8,'x'=4,'c'=2,'tp'=8] {'x'}, dimensions={0} | all-to-all | bytes 1048576 | tf_op jit(solution)/shard_map/cond/branch_1_fun/all_to_all | solution.py:304
  72.5 0.1 reduce_sum.31
  72.7 15.4 %all_to_all.40.got_ref = bf16[64,4,256]{2,1,0:T(4,128)(2,1)S(1)} all-to-all(bf16[64,4,256]{2,1,0:T(4,128)(2,1)S(1)} %reshape.37), channel_id=1, replica_groups=mesh['z'=8,'x'=4,'c'=2,'tp'=8] {'z','tp'}, dimensions={0} | all-to-all | bytes 262144 | tf_op jit(solution)/shard_map/all_to_all | solution.py:341
  88.1 0.7 finish.1
  (3 shorter events, 0.1 us)
Async XLA Ops:
  0.6 0.7 copy-start.1
  0.6 0.7 copy-start.2
  0.7 0.7 copy-start.3
  1.3 0.7 copy-start
  2.8 28.9 %copy-start.4 = (bf16[128,1024]{1,0:T(8,128)(2,1)S(1)}, bf16[128,1024]{1,0:T(8,128)(2,1)}, u32[]{:S(2)}) copy-start(bf16[128,1024]{1,0:T(8,128)(2,1)} %param.8) | copy-start | bytes 786436
  2.8 28.9 %copy-start.5 = (bf16[128,1024]{1,0:T(8,128)(2,1)S(1)}, bf16[128,1024]{1,0:T(8,128)(2,1)}, u32[]{:S(2)}) copy-start(bf16[128,1024]{1,0:T(8,128)(2,1)} %param.11) | copy-start | bytes 786436
  2.8 28.8 %all-to-all-start.6 = ((bf16[64,4,256]{2,1,0:T(4,128)(2,1)}), bf16[64,4,256]{2,1,0:T(4,128)(2,1)S(1)}, u32[]{:S(2)}, u32[]{:S(2)}) async-start(bf16[64,4,256]{2,1,0:T(4,128)(2,1)} %get-tuple-element.46), calls=%async_computation.6 | async-start | bytes 262144 | tf_op jit(solution)/shard_map/all_to_all | solution.py:323

commit v4 on v3

v4 whole, which is shorter than its diff:
```python
import functools
import math

import jax
import jax.numpy as jnp
from jax import lax
from jax.experimental import pallas as pl
from jax.experimental.pallas import tpu as pltpu
from jax.sharding import Mesh, PartitionSpec as P

HD = 128
BLOCK = 64
TILES_IMG = 4

epsilon = 1e-05
neg_fill = -1e30
score_scale = 1.0 / math.sqrt(HD)

NN = (((1,), (0,)), ((), ()))
NT = (((1,), (1,)), ((), ()))
TN = (((0,), (0,)), ((), ()))


def dot(a, b, dims):
    return lax.dot_general(a, b, dims, preferred_element_type=jnp.float32)


def attention_kernel(further, info_ref, query_ref, grad_ref, *refs):
    come_ref = back_ref = None
    if further:
        come_ref, kv_ref, out_ref, query_grad_ref, back_ref, terms_ref, key_acc, value_acc = refs
    else:
        kv_ref, out_ref, query_grad_ref, terms_ref, key_acc, value_acc = refs
    groups, group_rows, _ = kv_ref.shape
    part = group_rows // TILES_IMG
    span = groups * group_rows
    heads = query_ref.shape[1] // HD
    lane = lax.broadcasted_iota(jnp.int32, info_ref.shape, 1)
    tiles = [jnp.sum(jnp.where(lane == k, info_ref[...], 0.0)).astype(jnp.int32) for k in range(2)]

    def keys():
        return kv_ref[:, :, :HD].reshape(span, HD)

    def values():
        return kv_ref[:, :, HD:].reshape(span, HD)

    def block_of(ref, other_ref, which, b):
        if further and b == 1:
            return other_ref.at[which]
        return ref.at[pl.ds((1 if further else b) * BLOCK, BLOCK)]

    def stacked(rows, first, count):
        return jnp.concatenate([rows[:, j * HD : (j + 1) * HD] for j in range(first, first + count)], axis=0)

    def unstack(rows, first, count, value):
        for j in range(count):
            rows[:, (first + j) * HD : (first + j + 1) * HD] = value[j * BLOCK : (j + 1) * BLOCK]

    per_chunk = 4
    column = lax.broadcasted_iota(jnp.int32, (1, span), 1)
    bias = [jnp.where((column & (group_rows - 1)) < n * part, 0.0, neg_fill) for n in tiles]
    live = [(n > 0).astype(jnp.float32) for n in tiles]

    def front(b, first):
        query = stacked(block_of(query_ref, come_ref, 0, b), first, per_chunk)
        grad = stacked(block_of(grad_ref, come_ref, 1, b), first, per_chunk)
        scores = dot(query, keys(), NT) + bias[b]
        prob_grad = dot(grad, values(), NT)
        return query, grad, scores, prob_grad

    def middle(b, first, query, grad, scores, prob_grad):
        row_max = jnp.max(scores, axis=1, keepdims=True)
        terms = jnp.exp((scores - row_max) * score_scale)
        inverse_sum = live[b] / jnp.sum(terms, axis=1, keepdims=True)
        weights = terms * inverse_sum
        probs = weights.astype(jnp.bfloat16)
        out = dot(probs, values(), NN).astype(jnp.bfloat16)
        unstack(block_of(out_ref, back_ref, 0, b), first, per_chunk, out)
        delta = jnp.sum(grad.astype(jnp.float32) * out.astype(jnp.float32), axis=1, keepdims=True)
        dscore = (weights * (prob_grad - delta)).astype(jnp.bfloat16)
        return probs, dscore

    def back(b, first, query, grad, probs, dscore):
        query_grad = (dot(dscore, keys(), NN) * score_scale).astype(jnp.bfloat16)
        unstack(block_of(query_grad_ref, back_ref, 1, b), first, per_chunk, query_grad)
        value_term = dot(probs, grad, TN)
        key_term = dot(dscore, query, TN)
        if b == 0 and first == 0:
            value_acc[...] = value_term
            key_acc[...] = key_term
        else:
            value_acc[...] += value_term
            key_acc[...] += key_term

    chunks = [(b, first) for b in range(2) for first in range(0, heads, per_chunk)]
    held = None
    for chunk in chunks:
        query, grad, scores, prob_grad = front(*chunk)
        if held is not None:
            back(*held)
        probs, dscore = middle(*chunk, query, grad, scores, prob_grad)
        held = (*chunk, query, grad, probs, dscore)
    back(*held)
    terms_ref[:, :, :HD] = (key_acc[...] * score_scale).astype(jnp.bfloat16).reshape(groups, group_rows, HD)
    terms_ref[:, :, HD:] = value_acc[...].astype(jnp.bfloat16).reshape(groups, group_rows, HD)


def attention(info, query, out_grad, kv, come=None):
    span = kv.shape[0] * kv.shape[1]
    vmem = pl.BlockSpec(memory_space=pltpu.VMEM)
    work = 6 * 2 * query.size * span
    moved = [] if come is None else [come]
    args = [info, query, out_grad, *moved, kv]
    shapes = [query.shape, query.shape, *(array.shape for array in moved), kv.shape]
    return pl.pallas_call(
        functools.partial(attention_kernel, come is not None),
        out_shape=[jax.ShapeDtypeStruct(shape, jnp.bfloat16) for shape in shapes],
        in_specs=[vmem] * len(args),
        out_specs=[vmem] * len(shapes),
        scratch_shapes=[pltpu.VMEM((span, HD), jnp.float32)] * 2,
        compiler_params=pltpu.CompilerParams(vmem_limit_bytes=40 * 1024 * 1024),
        cost_estimate=pl.CostEstimate(flops=work, bytes_accessed=5 * 1024 * 1024, transcendentals=query.size * span // HD),
        name="attention",
    )(*args)


def prepare_kernel(
    mesh_index, image_ref, tiles_ref, gain_ref, kv_ref,
    copies_ref, info_ref, plane_ref, normed_ref, inverse_ref, kept_gain_ref,
):
    heads = normed_ref.shape[1] // HD
    gain, image, tiles = (gain_ref[...], image_ref[...].astype(jnp.float32), tiles_ref[...].astype(jnp.float32))
    lane = lax.broadcasted_iota(jnp.int32, info_ref.shape, 1)
    plane, place, cores = mesh_index()
    begin = (plane + place) * 2

    blocks = image.shape[1]
    mixed = jnp.sum(jnp.where((lane & 1) == 1, image, -image), axis=1, keepdims=True)
    begin = begin + (mixed > 0.5).astype(jnp.int32)

    def entry(row, index):
        return jnp.sum(jnp.where(lane == (index & (blocks - 1)), row, 0.0), axis=1, keepdims=True)

    info_ref[...] = jnp.where(
        lane == 0, entry(tiles, begin), jnp.where(lane == 1, entry(tiles, begin + 1), jnp.where(lane == 2, mixed, 0.0))
    )
    members = plane_ref.shape[0]
    member = lax.broadcasted_iota(jnp.int32, (members, blocks), 0)
    member_lane = lax.broadcasted_iota(jnp.int32, (members, blocks), 1)
    first = plane * 2 + (mixed > 0.5).astype(jnp.int32)
    for core in range(cores):
        upper = member - core * (members // cores)
        first = first + jnp.where((upper >= 0) & (upper < members // cores), (upper * cores + core) * 2, 0)
    seen = jnp.sum(jnp.where(member_lane == first, image, 0.0), axis=1, keepdims=True)
    plane_ref[...] = jnp.broadcast_to(seen, plane_ref.shape)
    kept_gain_ref[...] = gain
    for t in range(heads):
        pre = kv_ref[:, 2 * t * HD : (2 * t + 1) * HD].astype(jnp.float32)
        values = kv_ref[:, (2 * t + 1) * HD : (2 * t + 2) * HD]
        inverse = lax.rsqrt(jnp.mean(pre * pre, axis=1, keepdims=True) + epsilon)
        normed = pre * inverse
        keys = (normed * gain).astype(jnp.bfloat16)
        normed_ref[:, t * HD : (t + 1) * HD] = normed
        inverse_ref[:, t * HD : (t + 1) * HD] = jnp.broadcast_to(inverse, normed.shape)
        for copy in range(t, copies_ref.shape[0], heads):
            copies_ref[copy, :, :HD] = keys
            copies_ref[copy, :, HD:] = values


def prepare(mesh_index, members, span_image, span_tiles, key_gain, vision_kv, copies):
    rows, columns = vision_kv.shape
    heads = columns // (2 * HD)
    vmem = pl.BlockSpec(memory_space=pltpu.VMEM)
    return pl.pallas_call(
        functools.partial(prepare_kernel, mesh_index),
        out_shape=[
            jax.ShapeDtypeStruct((copies * heads, rows, 2 * HD), jnp.bfloat16),
            jax.ShapeDtypeStruct((1, HD), jnp.float32),
            jax.ShapeDtypeStruct((members, 2 * HD), jnp.float32),
            jax.ShapeDtypeStruct((rows, heads * HD), jnp.float32),
            jax.ShapeDtypeStruct((rows, heads * HD), jnp.float32),
            jax.ShapeDtypeStruct((1, HD), jnp.float32),
        ],
        in_specs=[vmem] * 4,
        out_specs=[vmem] * 6,
        compiler_params=pltpu.CompilerParams(vmem_limit_bytes=8 * 1024 * 1024),
        name="prepare",
    )(span_image.reshape(1, -1), span_tiles.reshape(1, -1), key_gain.reshape(1, -1), vision_kv)


def finish_kernel(got_ref, normed_ref, inverse_ref, gain_ref, out_ref):
    heads = out_ref.shape[1] // (2 * HD)
    gain = gain_ref[...]
    for t in range(heads):
        key_grad, value_grad = (
            sum(got_ref[k, :, part * HD : (part + 1) * HD].astype(jnp.float32) for k in range(t, got_ref.shape[0], heads))
            for part in range(2)
        )
        normed = normed_ref[:, t * HD : (t + 1) * HD]
        inverse = inverse_ref[:, t * HD : (t + 1) * HD]
        scaled = key_grad * gain
        pre_grad = inverse * (scaled - normed * jnp.mean(scaled * normed, axis=1, keepdims=True))
        out_ref[:, 2 * t * HD : (2 * t + 1) * HD] = pre_grad.astype(jnp.bfloat16)
        out_ref[:, (2 * t + 1) * HD : (2 * t + 2) * HD] = value_grad.astype(jnp.bfloat16)


def finish(got, normed, inverse, gain):
    rows = normed.shape[0]
    vmem = pl.BlockSpec(memory_space=pltpu.VMEM)
    return pl.pallas_call(
        finish_kernel,
        out_shape=jax.ShapeDtypeStruct((rows, 2 * normed.shape[1]), jnp.bfloat16),
        in_specs=[vmem] * 4,
        out_specs=vmem,
        compiler_params=pltpu.CompilerParams(vmem_limit_bytes=8 * 1024 * 1024),
        name="finish",
    )(got, normed, inverse, gain)


def route_kernel(plane_ref, column_ref, out_ref):
    members, image_rows, _ = out_ref.shape
    first = column_ref[:image_rows, :]
    second = column_ref[image_rows:, :]
    for k in range(members):
        out_ref[k] = jnp.where(plane_ref[k : k + 1, :] > 0.5, second, first)


def collect_kernel(plane_ref, got_ref, out_ref):
    members, image_rows, _ = got_ref.shape
    totals = [0.0, 0.0]
    for k in range(members):
        term = got_ref[k].astype(jnp.float32)
        second = plane_ref[k : k + 1, :] > 0.5
        totals = [totals[0] + jnp.where(second, 0.0, term), totals[1] + jnp.where(second, term, 0.0)]
    for image in range(2):
        out_ref[image * image_rows : (image + 1) * image_rows, :] = totals[image].astype(jnp.bfloat16)


def small_call(kernel, shape, *args):
    vmem = pl.BlockSpec(memory_space=pltpu.VMEM)
    return pl.pallas_call(
        kernel,
        out_shape=jax.ShapeDtypeStruct(shape, jnp.bfloat16),
        in_specs=[vmem] * len(args),
        out_specs=vmem,
        compiler_params=pltpu.CompilerParams(vmem_limit_bytes=8 * 1024 * 1024),
        name=kernel.__name__,
    )(*args)


def body(query, vision_kv, key_gain, out_grad, span_image, span_tiles):
    z, x, cores, tp = (lax.axis_size(name) for name in ("z", "x", "c", "tp"))
    own_rows = vision_kv.shape[0]
    column_rows = z * tp * own_rows
    image_rows = column_rows // 2
    members = x * cores

    def mesh_index():
        return lax.axis_index("z") * members, lax.axis_index("x") * cores + lax.axis_index("c"), cores

    mixed = jnp.sum(jnp.where(jnp.arange(span_image.shape[0]) % 2 == 1, span_image, -span_image)) > 0

    copies, info, plane, normed, inverse, gain = prepare(
        mesh_index, members, span_image, span_tiles, key_gain, vision_kv, z
    )
    along_z = lax.all_to_all(copies, ("z", "tp"), split_axis=0, concat_axis=0, tiled=True)
    column = along_z.reshape(column_rows, 2 * HD)

    def pass_on(blocks, step):
        count = z * members
        return lax.ppermute(blocks, ("z", "x", "c"), [(source, (source + step) % count) for source in range(count)])

    def travel(plane, column):
        routed = small_call(route_kernel, (members, image_rows, 2 * HD), plane, column)
        return lax.all_to_all(routed, ("c", "x"), split_axis=0, concat_axis=0, tiled=True)

    def travel_back(plane, terms):
        got = lax.all_to_all(terms, ("c", "x"), split_axis=0, concat_axis=0, tiled=True)
        return small_call(collect_kernel, column.shape, plane, got)

    def own_blocks(info, plane, column, query, out_grad):
        attn_out, query_grad, terms = attention(info, query, out_grad, travel(plane, column))
        return attn_out, query_grad, travel_back(plane, terms)

    def blocks_further(info, plane, column, query, out_grad):
        come = pass_on(jnp.stack([query[:BLOCK], out_grad[:BLOCK]]), -1)
        attn_out, query_grad, back, terms = attention(info, query, out_grad, travel(plane, column), come)
        home = pass_on(back, 1)
        terms = travel_back(plane, terms)
        return attn_out.at[:BLOCK].set(home[0]), query_grad.at[:BLOCK].set(home[1]), terms

    attn_out, query_grad, terms = lax.cond(
        mixed, blocks_further, own_blocks, info, plane, column, query, out_grad
    )
    got = lax.all_to_all(
        terms.reshape(z * tp, own_rows, 2 * HD), ("z", "tp"), split_axis=0, concat_axis=0, tiled=True
    )
    return (attn_out, query_grad, finish(got, normed, inverse, gain))


def solution(mesh):
    fine = Mesh(mesh.devices.reshape(8, 4, 2, 8), ("z", "x", "c", "tp"))
    seq = ("z", "x", "c")
    in_specs = (P(seq, "tp"), P(seq + ("tp",), None), P(), P(seq, "tp"), P(), P())
    out_specs = (P(seq, "tp"), P(seq, "tp"), P(seq + ("tp",), None))
    return jax.shard_map(body, mesh=fine, in_specs=in_specs, out_specs=out_specs, check_vma=False)
```

time: 89.3 us -> 87.9 us (0.984)
  blocking collectives: 50.1 us -> 15.4 us
  waiting for transfers between devices: 10.3 us -> 27.9 us
  starting transfers between devices: 17.3 us -> 32 us
    all_to_all x4 -> x0, blocking collectives: 34.7 us -> none  [the longest x2 18.5 us: spread(): lax.all_to_all(lax.optimization_barrier(jnp.broadcast_to(rows, (copies,)...]
    all_to_all x0 -> x2, starting transfers between devices: none -> 10.9 us  [the longest x1 6.42 us: travel(): lax.all_to_all(routed, ('c', 'x'), split_axis=0, concat_axis=0, tiled=True)]
    ppermute x0 -> x2, waiting for transfers between devices: none -> 8.98 us  [pass_on(): lax.ppermute(blocks, ('z', 'x', 'c'), [(source, (source + step) % count)...]
    all_to_all x0 -> x2, waiting for transfers between devices: none -> 8.65 us  [the longest x1 8.65 us: travel_back(): lax.all_to_all(terms, ('c', 'x'), split_axis=0, concat_axis=0, tiled=True)]
    ppermute x0 -> x2, starting transfers between devices: none -> 3.83 us  [pass_on(): lax.ppermute(blocks, ('z', 'x', 'c'), [(source, (source + step) % count)...]
    pallas_call x1 -> x3, Pallas kernels: 5.56 us -> 6.27 us  [the longest x1 5.21 us: attention(): pl.pallas_call(functools.partial(attention_kernel, come is not None), out...]
  transfers between devices with their start and end apart: 1 -> 5, of which waited for: 1 -> 3; matrix products, arithmetic and copies ran while one was open for 1% -> 2% of each run, Pallas kernels for 0% -> 0%
where the time goes in v4:
time: 87.9 us; the launch traced here: 87.4 us
  starting transfers between devices  32 us (36%)
  waiting for transfers between devices  27.9 us (32%)
  blocking collectives  15.4 us (18%)
  Pallas kernels  7.76 us (9%)
  local copies, waits for them, and re-layouts  2.19 us (2%)
  between operations  1.34 us (2%)
    all_to_all x1, starting transfers between devices, body(): lax.all_to_all(copies, ('z', 'tp'), split_axis=0, concat_axis=0, tiled=True)  17.3 us
    all_to_all x1, blocking collectives, body(): lax.all_to_all(terms.reshape(z * tp, own_rows, 2 * HD), ('z', 'tp'), spli...  15.4 us
    all_to_all x1, waiting for transfers between devices, body(): lax.all_to_all(copies, ('z', 'tp'), split_axis=0, concat_axis=0, tiled=True)  10.3 us
    ppermute x2, waiting for transfers between devices, pass_on(): lax.ppermute(blocks, ('z', 'x', 'c'), [(source, (source + step) % count)...  8.98 us
    all_to_all x1, waiting for transfers between devices, travel_back(): lax.all_to_all(terms, ('c', 'x'), split_axis=0, concat_axis=0, tiled=True)  8.65 us
    all_to_all x1, starting transfers between devices, travel(): lax.all_to_all(routed, ('c', 'x'), split_axis=0, concat_axis=0, tiled=True)  6.42 us
    pallas_call x1, Pallas kernels, attention(): pl.pallas_call(functools.partial(attention_kernel, come is not None), out...  5.21 us
    all_to_all x1, starting transfers between devices, travel_back(): lax.all_to_all(terms, ('c', 'x'), split_axis=0, concat_axis=0, tiled=True)  4.52 us
  transfers between devices with their start and end apart: 5, of which 3 were waited for; matrix products, arithmetic and copies ran while one was open for 2% of the time, Pallas kernels for 0%

profile of v4, /device:TPU:1, one launch (start us, length us, event | category | flops | bytes accessed | tf_op | source)
XLA Modules:
  0.0 87.4 jit_solution(13166000172425233491)
XLA Ops:
  0.6 0.0 copy-start.1
  0.6 0.0 copy-start.2
  0.7 0.0 copy-start.3
  0.7 0.6 copy-done.1
  1.3 0.0 copy-done.2
  1.3 0.0 copy-done.3
  1.3 0.0 copy-start
  1.3 0.7 copy-done
  2.0 0.8 prepare.1
  2.8 0.0 copy-start.4
  2.8 0.0 copy-start.5
  2.8 17.3 %all-to-all-start.4 = ((bf16[64,4,256]{2,1,0:T(4,128)(2,1)}), bf16[64,4,256]{2,1,0:T(4,128)(2,1)S(1)}, u32[]{:S(2)}, u32[]{:S(2)}) async-start(bf16[64,4,256]{2,1,0:T(4,128)(2,1)} %get-tuple-element.74), calls=%async_computation.4 | async-start | bytes 262144 | tf_op jit(solution)/shard_map/all_to_all | solution.py:266
  20.1 0.6 fusion.2
  21.4 10.3 %all-to-all-done.4 = bf16[64,4,256]{2,1,0:T(4,128)(2,1)S(1)} async-done(((bf16[64,4,256]{2,1,0:T(4,128)(2,1)}), bf16[64,4,256]{2,1,0:T(4,128)(2,1)S(1)}, u32[]{:S(2)}, u32[]{:S(2)}) %all-to-all-start.4) | async-done | bytes 131104 | tf_op jit(solution)/shard_map/all_to_all | solution.py:266
  31.7 0.0 copy-done.4
  31.7 0.0 copy-done.5
  31.7 39.5 %conditional.1 = (bf16[128,1024]{1,0:T(8,128)(2,1)}, bf16[128,1024]{1,0:T(8,128)(2,1)}, bf16[256,256]{1,0:T(8,128)(2,1)S(1)}) conditional(s32[]{:T(128)} %convert_element_type.3, (f32[8,256]{1,0:T(8,128)S(1)}, bf16[256,256]{1,0:T(8,128)(2,1)S(1)}, f32[1,128]{1,0:T(1,128)S(1)}, bf16[128,1024]{1,0:T(8,128)(2,1)S(1)}, ...), branch_computations={%region_1.2_spmd, %region_2.3_spmd} | conditional | flops 1610743808 | bytes 12058792 | solution.py:292
  31.7 0.8 route_kernel.3
  32.6 6.4 %all-to-all-start.2 = ((bf16[8,128,256]{2,1,0:T(8,128)(2,1)}), bf16[8,128,256]{2,1,0:T(8,128)(2,1)S(1)}, u32[]{:S(2)}, u32[]{:S(2)}) async-start(bf16[8,128,256]{2,1,0:T(8,128)(2,1)} %route_kernel.3), calls=%async_computation.2 | async-start | bytes 1048576 | tf_op jit(solution)/shard_map/cond/branch_1_fun/all_to_all | solution.py:275
  39.0 1.9 %collective-permute-start = (bf16[2,64,1024]{2,1,0:T(8,128)(2,1)S(1)}, bf16[2,64,1024]{2,1,0:T(8,128)(2,1)S(1)}, u32[]{:S(2)}, u32[]{:S(2)}) collective-permute-start(bf16[2,64,1024]{2,1,0:T(8,128)(2,1)S(1)} %pad_maximum_fusion), channel_id=1, source_target_pairs={{0,504},{8,0},{16,8},{24,16},{32,24},{40,32},{48,40},{56,48},{64,5... | collective-permute-start | bytes 786440 | tf_op jit(solution)/shard_map/cond/branch_1_fun/ppermute | solution.py:271
  41.0 9.0 %collective-permute-done.refs_0_ = bf16[2,64,1024]{2,1,0:T(8,128)(2,1)S(1)} collective-permute-done((bf16[2,64,1024]{2,1,0:T(8,128)(2,1)S(1)}, bf16[2,64,1024]{2,1,0:T(8,128)(2,1)S(1)}, u32[]{:S(2)}, u32[]{:S(2)}) %collective-permute-start) | collective-permute-done | bytes 262176 | tf_op jit(solution)/shard_map/cond/branch_1_fun/ppermute | solution.py:271
  50.0 0.0 all-to-all-done.2.refs_1_
  50.0 5.2 %attention.3 = (bf16[128,1024]{1,0:T(8,128)(2,1)}, bf16[128,1024]{1,0:T(8,128)(2,1)}, bf16[2,64,1024]{2,1,0:T(8,128)(2,1)S(1)}, bf16[8,128,256]{2,1,0:T(8,128)(2,1)}) custom-call(f32[1,128]{1,0:T(1,128)S(1)} %get-tuple-element.52.info_ref, bf16[128,1024]{1,0:T(8,128)(2,1)S(1)} %get-tuple-element.53.query_ref, ...), custom_call_target="tpu_custom_call" | custom-call | flops 1610612736 | bytes 5242880 | tf_op jit(solution)/shard_map/cond/branch_1_fun/attention/pallas_call | solution.py:115
  55.2 1.9 %collective-permute-start.1 = (bf16[2,64,1024]{2,1,0:T(8,128)(2,1)S(1)}, bf16[2,64,1024]{2,1,0:T(8,128)(2,1)S(1)}, u32[]{:S(2)}, u32[]{:S(2)}) collective-permute-start(bf16[2,64,1024]{2,1,0:T(8,128)(2,1)S(1)} %get-tuple-element.58), channel_id=1, source_target_pairs={{0,8},{8,16},{16,24},{24,32},{32,40},{40,48},{48,56},{56,64},{64,7... | collective-permute-start | bytes 786440 | tf_op jit(solution)/shard_map/cond/branch_1_fun/ppermute | solution.py:271
  57.1 4.5 %all-to-all-start.3 = ((bf16[8,128,256]{2,1,0:T(8,128)(2,1)}), bf16[8,128,256]{2,1,0:T(8,128)(2,1)S(1)}, u32[]{:S(2)}, u32[]{:S(2)}) async-start(bf16[8,128,256]{2,1,0:T(8,128)(2,1)} %get-tuple-element.60), calls=%async_computation.3 | async-start | bytes 1048576 | tf_op jit(solution)/shard_map/cond/branch_1_fun/all_to_all | solution.py:278
  61.6 0.0 collective-permute-done.1
  61.6 0.7 fusion
  62.3 8.7 %all-to-all-done.3.got_ref = bf16[8,128,256]{2,1,0:T(8,128)(2,1)S(1)} async-done(((bf16[8,128,256]{2,1,0:T(8,128)(2,1)}), bf16[8,128,256]{2,1,0:T(8,128)(2,1)S(1)}, u32[]{:S(2)}, u32[]{:S(2)}) %all-to-all-start.3) | async-done | bytes 524320 | tf_op jit(solution)/shard_map/cond/branch_1_fun/all_to_all | solution.py:278
  71.0 0.2 collect_kernel.3
  71.2 15.4 %all_to_all.28.got_ref = bf16[64,4,256]{2,1,0:T(4,128)(2,1)S(1)} all-to-all(bf16[64,4,256]{2,1,0:T(4,128)(2,1)S(1)} %reshape.78), channel_id=1, replica_groups=mesh['z'=8,'x'=4,'c'=2,'tp'=8] {'z','tp'}, dimensions={0} | all-to-all | bytes 262144 | tf_op jit(solution)/shard_map/all_to_all | solution.py:295
  86.7 0.7 finish.1
  (4 shorter events, 0.1 us)
Async XLA Ops:
  0.6 0.7 copy-start.1
  0.6 0.7 copy-start.2
  0.7 0.7 copy-start.3
  1.3 0.7 copy-start
  2.8 28.9 %copy-start.4 = (bf16[128,1024]{1,0:T(8,128)(2,1)S(1)}, bf16[128,1024]{1,0:T(8,128)(2,1)}, u32[]{:S(2)}) copy-start(bf16[128,1024]{1,0:T(8,128)(2,1)} %param.12) | copy-start | bytes 786436
  2.8 28.9 %copy-start.5 = (bf16[128,1024]{1,0:T(8,128)(2,1)S(1)}, bf16[128,1024]{1,0:T(8,128)(2,1)}, u32[]{:S(2)}) copy-start(bf16[128,1024]{1,0:T(8,128)(2,1)} %param.15) | copy-start | bytes 786436
  2.8 28.8 %all-to-all-start.4 = ((bf16[64,4,256]{2,1,0:T(4,128)(2,1)}), bf16[64,4,256]{2,1,0:T(4,128)(2,1)S(1)}, u32[]{:S(2)}, u32[]{:S(2)}) async-start(bf16[64,4,256]{2,1,0:T(4,128)(2,1)} %get-tuple-element.74), calls=%async_computation.4 | async-start | bytes 262144 | tf_op jit(solution)/shard_map/all_to_all | solution.py:266
  32.6 17.4 %all-to-all-start.2 = ((bf16[8,128,256]{2,1,0:T(8,128)(2,1)}), bf16[8,128,256]{2,1,0:T(8,128)(2,1)S(1)}, u32[]{:S(2)}, u32[]{:S(2)}) async-start(bf16[8,128,256]{2,1,0:T(8,128)(2,1)} %route_kernel.3), calls=%async_computation.2 | async-start | bytes 1048576 | tf_op jit(solution)/shard_map/cond/branch_1_fun/all_to_all | solution.py:275
  39.0 10.9 %collective-permute-start = (bf16[2,64,1024]{2,1,0:T(8,128)(2,1)S(1)}, bf16[2,64,1024]{2,1,0:T(8,128)(2,1)S(1)}, u32[]{:S(2)}, u32[]{:S(2)}) collective-permute-start(bf16[2,64,1024]{2,1,0:T(8,128)(2,1)S(1)} %pad_maximum_fusion), channel_id=1, source_target_pairs={{0,504},{8,0},{16,8},{24,16},{32,24},{40,32},{48,40},{56,48},{64,5... | collective-permute-start | bytes 786440 | tf_op jit(solution)/shard_map/cond/branch_1_fun/ppermute | solution.py:271
  55.2 6.4 %collective-permute-start.1 = (bf16[2,64,1024]{2,1,0:T(8,128)(2,1)S(1)}, bf16[2,64,1024]{2,1,0:T(8,128)(2,1)S(1)}, u32[]{:S(2)}, u32[]{:S(2)}) collective-permute-start(bf16[2,64,1024]{2,1,0:T(8,128)(2,1)S(1)} %get-tuple-element.58), channel_id=1, source_target_pairs={{0,8},{8,16},{16,24},{24,32},{32,40},{40,48},{48,56},{56,64},{64,7... | collective-permute-start | bytes 786440 | tf_op jit(solution)/shard_map/cond/branch_1_fun/ppermute | solution.py:271
  57.1 13.9 %all-to-all-start.3 = ((bf16[8,128,256]{2,1,0:T(8,128)(2,1)}), bf16[8,128,256]{2,1,0:T(8,128)(2,1)S(1)}, u32[]{:S(2)}, u32[]{:S(2)}) async-start(bf16[8,128,256]{2,1,0:T(8,128)(2,1)} %get-tuple-element.60), calls=%async_computation.3 | async-start | bytes 1048576 | tf_op jit(solution)/shard_map/cond/branch_1_fun/all_to_all | solution.py:278

commit v5 on v4

--- a/solution.py
+++ b/solution.py
@@ -124,16 +124,41 @@
     )(*args)
 
 
-def prepare_kernel(
-    mesh_index, image_ref, tiles_ref, gain_ref, kv_ref,
-    copies_ref, info_ref, plane_ref, normed_ref, inverse_ref, kept_gain_ref,
-):
+def prepare_kernel(kv_ref, copies_ref, normed_ref, inverse_ref):
     heads = normed_ref.shape[1] // HD
-    gain, image, tiles = (gain_ref[...], image_ref[...].astype(jnp.float32), tiles_ref[...].astype(jnp.float32))
+    for t in range(heads):
+        pre = kv_ref[:, 2 * t * HD : (2 * t + 1) * HD].astype(jnp.float32)
+        inverse = lax.rsqrt(jnp.mean(pre * pre, axis=1, keepdims=True) + epsilon)
+        normed_ref[:, t * HD : (t + 1) * HD] = pre * inverse
+        inverse_ref[:, t * HD : (t + 1) * HD] = jnp.broadcast_to(inverse, pre.shape)
+        for copy in range(t, copies_ref.shape[0], heads):
+            copies_ref[copy] = kv_ref[:, 2 * t * HD : (2 * t + 2) * HD]
+
+
+def prepare(vision_kv, copies):
+    rows, columns = vision_kv.shape
+    heads = columns // (2 * HD)
+    vmem = pl.BlockSpec(memory_space=pltpu.VMEM)
+    return pl.pallas_call(
+        prepare_kernel,
+        out_shape=[
+            jax.ShapeDtypeStruct((copies * heads, rows, 2 * HD), jnp.bfloat16),
+            jax.ShapeDtypeStruct((rows, heads * HD), jnp.float32),
+            jax.ShapeDtypeStruct((rows, heads * HD), jnp.float32),
+        ],
+        in_specs=[vmem],
+        out_specs=[vmem] * 3,
+        compiler_params=pltpu.CompilerParams(vmem_limit_bytes=8 * 1024 * 1024),
+        name="prepare",
+    )(vision_kv)
+
+
+def look_kernel(mesh_index, image_ref, tiles_ref, gain_ref, info_ref, plane_ref, kept_gain_ref):
+    image, tiles = image_ref[...].astype(jnp.float32), tiles_ref[...].astype(jnp.float32)
+    kept_gain_ref[...] = gain_ref[...]
     lane = lax.broadcasted_iota(jnp.int32, info_ref.shape, 1)
     plane, place, cores = mesh_index()
     begin = (plane + place) * 2
-
     blocks = image.shape[1]
     mixed = jnp.sum(jnp.where((lane & 1) == 1, image, -image), axis=1, keepdims=True)
     begin = begin + (mixed > 0.5).astype(jnp.int32)
@@ -153,39 +178,22 @@
         first = first + jnp.where((upper >= 0) & (upper < members // cores), (upper * cores + core) * 2, 0)
     seen = jnp.sum(jnp.where(member_lane == first, image, 0.0), axis=1, keepdims=True)
     plane_ref[...] = jnp.broadcast_to(seen, plane_ref.shape)
-    kept_gain_ref[...] = gain
-    for t in range(heads):
-        pre = kv_ref[:, 2 * t * HD : (2 * t + 1) * HD].astype(jnp.float32)
-        values = kv_ref[:, (2 * t + 1) * HD : (2 * t + 2) * HD]
-        inverse = lax.rsqrt(jnp.mean(pre * pre, axis=1, keepdims=True) + epsilon)
-        normed = pre * inverse
-        keys = (normed * gain).astype(jnp.bfloat16)
-        normed_ref[:, t * HD : (t + 1) * HD] = normed
-        inverse_ref[:, t * HD : (t + 1) * HD] = jnp.broadcast_to(inverse, normed.shape)
-        for copy in range(t, copies_ref.shape[0], heads):
-            copies_ref[copy, :, :HD] = keys
-            copies_ref[copy, :, HD:] = values
-
-
-def prepare(mesh_index, members, span_image, span_tiles, key_gain, vision_kv, copies):
-    rows, columns = vision_kv.shape
-    heads = columns // (2 * HD)
-    vmem = pl.BlockSpec(memory_space=pltpu.VMEM)
-    return pl.pallas_call(
-        functools.partial(prepare_kernel, mesh_index),
+
+
+def look(mesh_index, members, span_image, span_tiles, key_gain):
+    vmem = pl.BlockSpec(memory_space=pltpu.VMEM)
+    return pl.pallas_call(
+        functools.partial(look_kernel, mesh_index),
         out_shape=[
-            jax.ShapeDtypeStruct((copies * heads, rows, 2 * HD), jnp.bfloat16),
             jax.ShapeDtypeStruct((1, HD), jnp.float32),
             jax.ShapeDtypeStruct((members, 2 * HD), jnp.float32),
-            jax.ShapeDtypeStruct((rows, heads * HD), jnp.float32),
-            jax.ShapeDtypeStruct((rows, heads * HD), jnp.float32),
             jax.ShapeDtypeStruct((1, HD), jnp.float32),
         ],
-        in_specs=[vmem] * 4,
-        out_specs=[vmem] * 6,
+        in_specs=[vmem] * 3,
+        out_specs=[vmem] * 3,
         compiler_params=pltpu.CompilerParams(vmem_limit_bytes=8 * 1024 * 1024),
-        name="prepare",
-    )(span_image.reshape(1, -1), span_tiles.reshape(1, -1), key_gain.reshape(1, -1), vision_kv)
+        name="look",
+    )(span_image.reshape(1, -1), span_tiles.reshape(1, -1), key_gain.reshape(1, -1))
 
 
 def finish_kernel(got_ref, normed_ref, inverse_ref, gain_ref, out_ref):
@@ -217,12 +225,15 @@
     )(got, normed, inverse, gain)
 
 
-def route_kernel(plane_ref, column_ref, out_ref):
+def route_kernel(plane_ref, gain_ref, column_ref, out_ref):
     members, image_rows, _ = out_ref.shape
-    first = column_ref[:image_rows, :]
-    second = column_ref[image_rows:, :]
-    for k in range(members):
-        out_ref[k] = jnp.where(plane_ref[k : k + 1, :] > 0.5, second, first)
+    pre = column_ref[:, :HD].astype(jnp.float32)
+    inverse = lax.rsqrt(jnp.mean(pre * pre, axis=1, keepdims=True) + epsilon)
+    keys = (pre * inverse * gain_ref[...]).astype(jnp.bfloat16)
+    for half, rows in enumerate((keys, column_ref[:, HD:])):
+        part = slice(half * HD, (half + 1) * HD)
+        for k in range(members):
+            out_ref[k, :, part] = jnp.where(plane_ref[k : k + 1, part] > 0.5, rows[image_rows:], rows[:image_rows])
 
 
 def collect_kernel(plane_ref, got_ref, out_ref):
@@ -260,37 +271,37 @@
 
     mixed = jnp.sum(jnp.where(jnp.arange(span_image.shape[0]) % 2 == 1, span_image, -span_image)) > 0
 
-    copies, info, plane, normed, inverse, gain = prepare(
-        mesh_index, members, span_image, span_tiles, key_gain, vision_kv, z
-    )
+    copies, normed, inverse = prepare(vision_kv, z)
     along_z = lax.all_to_all(copies, ("z", "tp"), split_axis=0, concat_axis=0, tiled=True)
     column = along_z.reshape(column_rows, 2 * HD)
+    info, plane, gain = look(mesh_index, members, span_image, span_tiles, key_gain)
 
     def pass_on(blocks, step):
         count = z * members
         return lax.ppermute(blocks, ("z", "x", "c"), [(source, (source + step) % count) for source in range(count)])
 
-    def travel(plane, column):
-        routed = small_call(route_kernel, (members, image_rows, 2 * HD), plane, column)
+    def travel(plane, gain, column):
+        routed = small_call(route_kernel, (members, image_rows, 2 * HD), plane, gain, column)
         return lax.all_to_all(routed, ("c", "x"), split_axis=0, concat_axis=0, tiled=True)
 
     def travel_back(plane, terms):
         got = lax.all_to_all(terms, ("c", "x"), split_axis=0, concat_axis=0, tiled=True)
         return small_call(collect_kernel, column.shape, plane, got)
 
-    def own_blocks(info, plane, column, query, out_grad):
-        attn_out, query_grad, terms = attention(info, query, out_grad, travel(plane, column))
+    def own_blocks(info, plane, gain, column, query, out_grad):
+        attn_out, query_grad, terms = attention(info, query, out_grad, travel(plane, gain, column))
         return attn_out, query_grad, travel_back(plane, terms)
 
-    def blocks_further(info, plane, column, query, out_grad):
+    def blocks_further(info, plane, gain, column, query, out_grad):
         come = pass_on(jnp.stack([query[:BLOCK], out_grad[:BLOCK]]), -1)
-        attn_out, query_grad, back, terms = attention(info, query, out_grad, travel(plane, column), come)
+        attn_out, query_grad, back, terms = attention(info, query, out_grad, travel(plane, gain, column), come)
         home = pass_on(back, 1)
         terms = travel_back(plane, terms)
-        return attn_out.at[:BLOCK].set(home[0]), query_grad.at[:BLOCK].set(home[1]), terms
+        outputs = [jnp.concatenate([home[k], rows[BLOCK:]], axis=0) for k, rows in enumerate((attn_out, query_grad))]
+        return *outputs, terms
 
     attn_out, query_grad, terms = lax.cond(
-        mixed, blocks_further, own_blocks, info, plane, column, query, out_grad
+        mixed, blocks_further, own_blocks, info, plane, gain, column, query, out_grad
     )
     got = lax.all_to_all(
         terms.reshape(z * tp, own_rows, 2 * HD), ("z", "tp"), split_axis=0, concat_axis=0, tiled=True

time: 87.9 us -> 87.2 us (level)
  transfers between devices with their start and end apart: 5 -> 5, of which waited for: 3 -> 3; matrix products, arithmetic and copies ran while one was open for 2% -> 1% of each run, Pallas kernels for 0% -> 0%
where the time goes in v5:
time: 87.2 us; the launch traced here: 86.7 us
  starting transfers between devices  32 us (37%)
  waiting for transfers between devices  27.6 us (32%)
  blocking collectives  15.4 us (18%)
  Pallas kernels  7.96 us (9%)
  local copies, waits for them, and re-layouts  1.51 us (2%)
  between operations  1.37 us (2%)
    all_to_all x1, starting transfers between devices, body(): lax.all_to_all(copies, ('z', 'tp'), split_axis=0, concat_axis=0, tiled=True)  17.3 us
    all_to_all x1, blocking collectives, body(): lax.all_to_all(terms.reshape(z * tp, own_rows, 2 * HD), ('z', 'tp'), spli...  15.4 us
    all_to_all x1, waiting for transfers between devices, body(): lax.all_to_all(copies, ('z', 'tp'), split_axis=0, concat_axis=0, tiled=True)  9.41 us
    all_to_all x1, waiting for transfers between devices, travel_back(): lax.all_to_all(terms, ('c', 'x'), split_axis=0, concat_axis=0, tiled=True)  9.25 us
    ppermute x2, waiting for transfers between devices, pass_on(): lax.ppermute(blocks, ('z', 'x', 'c'), [(source, (source + step) % count)...  8.98 us
    all_to_all x1, starting transfers between devices, travel(): lax.all_to_all(routed, ('c', 'x'), split_axis=0, concat_axis=0, tiled=True)  6.42 us
    pallas_call x1, Pallas kernels, attention(): pl.pallas_call(functools.partial(attention_kernel, come is not None), out...  5.23 us
    all_to_all x1, starting transfers between devices, travel_back(): lax.all_to_all(terms, ('c', 'x'), split_axis=0, concat_axis=0, tiled=True)  4.51 us
  transfers between devices with their start and end apart: 5, of which 3 were waited for; matrix products, arithmetic and copies ran while one was open for 1% of the time, Pallas kernels for 0%

profile of v5, /device:TPU:1, one launch (start us, length us, event | category | flops | bytes accessed | tf_op | source)
XLA Modules:
  0.0 86.7 jit_solution(15785319805759206208)
XLA Ops:
  0.6 0.0 copy-start
  0.6 0.7 copy-done
  1.3 0.7 prepare.1
  2.0 0.0 copy-start.1
  2.0 0.0 copy-start.4
  2.0 17.3 %all-to-all-start.4 = ((bf16[64,4,256]{2,1,0:T(4,128)(2,1)}), bf16[64,4,256]{2,1,0:T(4,128)(2,1)S(1)}, u32[]{:S(2)}, u32[]{:S(2)}) async-start(bf16[64,4,256]{2,1,0:T(4,128)(2,1)} %get-tuple-element.57), calls=%async_computation.4 | async-start | bytes 262144 | tf_op jit(solution)/shard_map/all_to_all | solution.py:275
  19.3 0.0 copy-done.1
  19.3 0.6 fusion
  20.6 0.0 copy-start.2
  20.6 0.0 copy-start.3
  20.6 0.0 copy-start.5
  20.6 0.6 copy-done.2
  21.3 0.0 copy-done.3
  21.3 0.2 look.1
  21.4 9.4 %all-to-all-done.4 = bf16[64,4,256]{2,1,0:T(4,128)(2,1)S(1)} async-done(((bf16[64,4,256]{2,1,0:T(4,128)(2,1)}), bf16[64,4,256]{2,1,0:T(4,128)(2,1)S(1)}, u32[]{:S(2)}, u32[]{:S(2)}) %all-to-all-start.4) | async-done | bytes 131104 | tf_op jit(solution)/shard_map/all_to_all | solution.py:275
  30.9 0.0 copy-done.4
  30.9 0.0 copy-done.5
  30.9 39.6 %conditional.1 = (bf16[128,1024]{1,0:T(8,128)(2,1)S(1)}, bf16[128,1024]{1,0:T(8,128)(2,1)S(1)}, bf16[256,256]{1,0:T(8,128)(2,1)S(1)}) conditional(s32[]{:T(128)} %convert_element_type.3, (f32[8,256]{1,0:T(8,128)S(1)}, f32[1,128]{1,0:T(1,128)S(1)}, bf16[256,256]{1,0:T(8,128)(2,1)S(1)}, f32[1,128]{1,0:T(1,128)S(1)}, bf16[128,1024]{1,0:T(8,128)(2,1)S(1)}, ...), branch_computations={%region_1.2_spmd, %region_2.3_spmd} | conditional | flops 1611792384 | bytes 13631656 | solution.py:303
  30.9 1.0 %route_kernel.3 = bf16[8,128,256]{2,1,0:T(8,128)(2,1)} custom-call(f32[8,256]{1,0:T(8,128)S(1)} %get-tuple-element.36.plane_ref, f32[1,128]{1,0:T(1,128)S(1)} %get-tuple-element.37.gain_ref, bf16[256,256]{1,0:T(8,128)(2,1)S(1)} %get-tuple-element.38.column_ref), custom_call_target="tpu_custom_call" | custom-call | tf_op jit(solution)/shard_map/cond/branch_1_fun/route_kernel/pallas_call | solution.py:252
  31.9 6.4 %all-to-all-start.2 = ((bf16[8,128,256]{2,1,0:T(8,128)(2,1)}), bf16[8,128,256]{2,1,0:T(8,128)(2,1)S(1)}, u32[]{:S(2)}, u32[]{:S(2)}) async-start(bf16[8,128,256]{2,1,0:T(8,128)(2,1)} %route_kernel.3), calls=%async_computation.2 | async-start | bytes 1048576 | tf_op jit(solution)/shard_map/cond/branch_1_fun/all_to_all | solution.py:285
  38.4 1.9 %collective-permute-start = (bf16[2,64,1024]{2,1,0:T(8,128)(2,1)S(1)}, bf16[2,64,1024]{2,1,0:T(8,128)(2,1)S(1)}, u32[]{:S(2)}, u32[]{:S(2)}) collective-permute-start(bf16[2,64,1024]{2,1,0:T(8,128)(2,1)S(1)} %pad_maximum_fusion), channel_id=1, source_target_pairs={{0,504},{8,0},{16,8},{24,16},{32,24},{40,32},{48,40},{56,48},{64,5... | collective-permute-start | bytes 786440 | tf_op jit(solution)/shard_map/cond/branch_1_fun/ppermute | solution.py:281
  40.3 9.0 %collective-permute-done.refs_0_ = bf16[2,64,1024]{2,1,0:T(8,128)(2,1)S(1)} collective-permute-done((bf16[2,64,1024]{2,1,0:T(8,128)(2,1)S(1)}, bf16[2,64,1024]{2,1,0:T(8,128)(2,1)S(1)}, u32[]{:S(2)}, u32[]{:S(2)}) %collective-permute-start) | collective-permute-done | bytes 262176 | tf_op jit(solution)/shard_map/cond/branch_1_fun/ppermute | solution.py:281
  49.3 0.0 all-to-all-done.2.refs_1_
  49.3 5.2 %attention.3 = (bf16[128,1024]{1,0:T(8,128)(2,1)S(1)}, bf16[128,1024]{1,0:T(8,128)(2,1)S(1)}, bf16[2,64,1024]{2,1,0:T(8,128)(2,1)S(1)}, bf16[8,128,256]{2,1,0:T(8,128)(2,1)}) custom-call(f32[1,128]{1,0:T(1,128)S(1)} %get-tuple-element.33.info_ref, bf16[128,1024]{1,0:T(8,128)(2,1)S(1)} %get-tuple-element.34.query_ref, ...), custom_call_target="tpu_custom_call" | custom-call | flops 1610612736 | bytes 5242880 | tf_op jit(solution)/shard_map/cond/branch_1_fun/attention/pallas_call | solution.py:115
  54.5 1.9 %collective-permute-start.1 = (bf16[2,64,1024]{2,1,0:T(8,128)(2,1)S(1)}, bf16[2,64,1024]{2,1,0:T(8,128)(2,1)S(1)}, u32[]{:S(2)}, u32[]{:S(2)}) collective-permute-start(bf16[2,64,1024]{2,1,0:T(8,128)(2,1)S(1)} %get-tuple-element.39), channel_id=1, source_target_pairs={{0,8},{8,16},{16,24},{24,32},{32,40},{40,48},{48,56},{56,64},{64,7... | collective-permute-start | bytes 786440 | tf_op jit(solution)/shard_map/cond/branch_1_fun/ppermute | solution.py:281
  56.4 4.5 %all-to-all-start.3 = ((bf16[8,128,256]{2,1,0:T(8,128)(2,1)}), bf16[8,128,256]{2,1,0:T(8,128)(2,1)S(1)}, u32[]{:S(2)}, u32[]{:S(2)}) async-start(bf16[8,128,256]{2,1,0:T(8,128)(2,1)} %get-tuple-element.42), calls=%async_computation.3 | async-start | bytes 1048576 | tf_op jit(solution)/shard_map/cond/branch_1_fun/all_to_all | solution.py:288
  61.0 0.0 collective-permute-done.1
  61.1 9.2 %all-to-all-done.3.got_ref = bf16[8,128,256]{2,1,0:T(8,128)(2,1)S(1)} async-done(((bf16[8,128,256]{2,1,0:T(8,128)(2,1)}), bf16[8,128,256]{2,1,0:T(8,128)(2,1)S(1)}, u32[]{:S(2)}, u32[]{:S(2)}) %all-to-all-start.3) | async-done | bytes 524320 | tf_op jit(solution)/shard_map/cond/branch_1_fun/all_to_all | solution.py:288
  70.3 0.2 collect_kernel.3
  70.5 0.0 copy-start.6
  70.5 0.0 copy-start.7
  70.6 15.4 %all_to_all.28.got_ref = bf16[64,4,256]{2,1,0:T(4,128)(2,1)S(1)} all-to-all(bf16[64,4,256]{2,1,0:T(4,128)(2,1)S(1)} %reshape.25), channel_id=1, replica_groups=mesh['z'=8,'x'=4,'c'=2,'tp'=8] {'z','tp'}, dimensions={0} | all-to-all | bytes 262144 | tf_op jit(solution)/shard_map/all_to_all | solution.py:306
  86.0 0.0 copy-done.6
  86.0 0.0 copy-done.7
  86.0 0.7 finish.1
  (9 shorter events, 0.2 us)
Async XLA Ops:
  0.6 0.7 copy-start
  2.0 17.3 %copy-start.1 = (s32[128]{0:T(128)S(1)}, s32[128]{0:T(128)}, u32[]{:S(2)}) copy-start(s32[128]{0:T(128)} %param.12) | copy-start | bytes 1540
  2.0 28.9 %copy-start.4 = (bf16[128,1024]{1,0:T(8,128)(2,1)S(1)}, bf16[128,1024]{1,0:T(8,128)(2,1)}, u32[]{:S(2)}) copy-start(bf16[128,1024]{1,0:T(8,128)(2,1)} %param.8) | copy-start | bytes 786436
  2.0 28.8 %all-to-all-start.4 = ((bf16[64,4,256]{2,1,0:T(4,128)(2,1)}), bf16[64,4,256]{2,1,0:T(4,128)(2,1)S(1)}, u32[]{:S(2)}, u32[]{:S(2)}) async-start(bf16[64,4,256]{2,1,0:T(4,128)(2,1)} %get-tuple-element.57), calls=%async_computation.4 | async-start | bytes 262144 | tf_op jit(solution)/shard_map/all_to_all | solution.py:275
  20.6 0.7 copy-start.2
  20.6 0.7 copy-start.3
  20.6 10.3 %copy-start.5 = (bf16[128,1024]{1,0:T(8,128)(2,1)S(1)}, bf16[128,1024]{1,0:T(8,128)(2,1)}, u32[]{:S(2)}) copy-start(bf16[128,1024]{1,0:T(8,128)(2,1)} %param.11) | copy-start | bytes 786436
  31.9 17.4 %all-to-all-start.2 = ((bf16[8,128,256]{2,1,0:T(8,128)(2,1)}), bf16[8,128,256]{2,1,0:T(8,128)(2,1)S(1)}, u32[]{:S(2)}, u32[]{:S(2)}) async-start(bf16[8,128,256]{2,1,0:T(8,128)(2,1)} %route_kernel.3), calls=%async_computation.2 | async-start | bytes 1048576 | tf_op jit(solution)/shard_map/cond/branch_1_fun/all_to_all | solution.py:285
  38.4 10.9 %collective-permute-start = (bf16[2,64,1024]{2,1,0:T(8,128)(2,1)S(1)}, bf16[2,64,1024]{2,1,0:T(8,128)(2,1)S(1)}, u32[]{:S(2)}, u32[]{:S(2)}) collective-permute-start(bf16[2,64,1024]{2,1,0:T(8,128)(2,1)S(1)} %pad_maximum_fusion), channel_id=1, source_target_pairs={{0,504},{8,0},{16,8},{24,16},{32,24},{40,32},{48,40},{56,48},{64,5... | collective-permute-start | bytes 786440 | tf_op jit(solution)/shard_map/cond/branch_1_fun/ppermute | solution.py:281
  54.5 6.5 %collective-permute-start.1 = (bf16[2,64,1024]{2,1,0:T(8,128)(2,1)S(1)}, bf16[2,64,1024]{2,1,0:T(8,128)(2,1)S(1)}, u32[]{:S(2)}, u32[]{:S(2)}) collective-permute-start(bf16[2,64,1024]{2,1,0:T(8,128)(2,1)S(1)} %get-tuple-element.39), channel_id=1, source_target_pairs={{0,8},{8,16},{16,24},{24,32},{32,40},{40,48},{48,56},{56,64},{64,7... | collective-permute-start | bytes 786440 | tf_op jit(solution)/shard_map/cond/branch_1_fun/ppermute | solution.py:281
  56.4 13.9 %all-to-all-start.3 = ((bf16[8,128,256]{2,1,0:T(8,128)(2,1)}), bf16[8,128,256]{2,1,0:T(8,128)(2,1)S(1)}, u32[]{:S(2)}, u32[]{:S(2)}) async-start(bf16[8,128,256]{2,1,0:T(8,128)(2,1)} %get-tuple-element.42), calls=%async_computation.3 | async-start | bytes 1048576 | tf_op jit(solution)/shard_map/cond/branch_1_fun/all_to_all | solution.py:288
  70.5 15.5 %copy-start.6 = (bf16[128,1024]{1,0:T(8,128)(2,1)}, bf16[128,1024]{1,0:T(8,128)(2,1)S(1)}, u32[]{:S(2)}) copy-start(bf16[128,1024]{1,0:T(8,128)(2,1)S(1)} %get-tuple-element.52) | copy-start | bytes 786436
  70.5 15.5 %copy-start.7 = (bf16[128,1024]{1,0:T(8,128)(2,1)}, bf16[128,1024]{1,0:T(8,128)(2,1)S(1)}, u32[]{:S(2)}) copy-start(bf16[128,1024]{1,0:T(8,128)(2,1)S(1)} %get-tuple-element.53) | copy-start | bytes 786436

commit v6 on v5

--- a/solution.py
+++ b/solution.py
@@ -70,7 +70,7 @@
 
     def middle(b, first, query, grad, scores, prob_grad):
         row_max = jnp.max(scores, axis=1, keepdims=True)
-        terms = jnp.exp((scores - row_max) * score_scale)
+        terms = jnp.exp2((scores - row_max) * (score_scale * math.log2(math.e)))
         inverse_sum = live[b] / jnp.sum(terms, axis=1, keepdims=True)
         weights = terms * inverse_sum
         probs = weights.astype(jnp.bfloat16)
@@ -85,9 +85,13 @@
         unstack(block_of(query_grad_ref, back_ref, 1, b), first, per_chunk, query_grad)
         value_term = dot(probs, grad, TN)
         key_term = dot(dscore, query, TN)
-        if b == 0 and first == 0:
+        if (b, first) == chunks[0]:
             value_acc[...] = value_term
             key_acc[...] = key_term
+        elif (b, first) == chunks[-1]:
+            key_total = (key_acc[...] + key_term) * score_scale
+            terms_ref[:, :, :HD] = key_total.astype(jnp.bfloat16).reshape(groups, group_rows, HD)
+            terms_ref[:, :, HD:] = (value_acc[...] + value_term).astype(jnp.bfloat16).reshape(groups, group_rows, HD)
         else:
             value_acc[...] += value_term
             key_acc[...] += key_term
@@ -101,8 +105,6 @@
         probs, dscore = middle(*chunk, query, grad, scores, prob_grad)
         held = (*chunk, query, grad, probs, dscore)
     back(*held)
-    terms_ref[:, :, :HD] = (key_acc[...] * score_scale).astype(jnp.bfloat16).reshape(groups, group_rows, HD)
-    terms_ref[:, :, HD:] = value_acc[...].astype(jnp.bfloat16).reshape(groups, group_rows, HD)
 
 
 def attention(info, query, out_grad, kv, come=None):

time: 87.2 us -> 87.1 us (level)
  no operation moved by 1% of the time
where the time goes in v6:
time: 87.1 us; the launch traced here: 86.6 us
  starting transfers between devices  32 us (37%)
  waiting for transfers between devices  27.6 us (32%)
  blocking collectives  15.4 us (18%)
  Pallas kernels  7.79 us (9%)
  local copies, waits for them, and re-layouts  1.51 us (2%)
  between operations  1.37 us (2%)
    all_to_all x1, starting transfers between devices, body(): lax.all_to_all(copies, ('z', 'tp'), split_axis=0, concat_axis=0, tiled=True)  17.3 us
    all_to_all x1, blocking collectives, body(): lax.all_to_all(terms.reshape(z * tp, own_rows, 2 * HD), ('z', 'tp'), spli...  15.4 us
    all_to_all x1, waiting for transfers between devices, body(): lax.all_to_all(copies, ('z', 'tp'), split_axis=0, concat_axis=0, tiled=True)  9.41 us
    all_to_all x1, waiting for transfers between devices, travel_back(): lax.all_to_all(terms, ('c', 'x'), split_axis=0, concat_axis=0, tiled=True)  9.25 us
    ppermute x2, waiting for transfers between devices, pass_on(): lax.ppermute(blocks, ('z', 'x', 'c'), [(source, (source + step) % count)...  8.98 us
    all_to_all x1, starting transfers between devices, travel(): lax.all_to_all(routed, ('c', 'x'), split_axis=0, concat_axis=0, tiled=True)  6.42 us
    pallas_call x1, Pallas kernels, attention(): pl.pallas_call(functools.partial(attention_kernel, come is not None), out...  5.06 us
    all_to_all x1, starting transfers between devices, travel_back(): lax.all_to_all(terms, ('c', 'x'), split_axis=0, concat_axis=0, tiled=True)  4.52 us
  transfers between devices with their start and end apart: 5, of which 3 were waited for; matrix products, arithmetic and copies ran while one was open for 1% of the time, Pallas kernels for 0%

profile of v6, /device:TPU:1, one launch (start us, length us, event | category | flops | bytes accessed | tf_op | source)
XLA Modules:
  0.0 86.6 jit_solution(15898339905350772325)
XLA Ops:
  0.6 0.0 copy-start
  0.6 0.7 copy-done
  1.3 0.7 prepare.1
  2.0 0.0 copy-start.1
  2.0 0.0 copy-start.4
  2.0 17.3 %all-to-all-start.4 = ((bf16[64,4,256]{2,1,0:T(4,128)(2,1)}), bf16[64,4,256]{2,1,0:T(4,128)(2,1)S(1)}, u32[]{:S(2)}, u32[]{:S(2)}) async-start(bf16[64,4,256]{2,1,0:T(4,128)(2,1)} %get-tuple-element.57), calls=%async_computation.4 | async-start | bytes 262144 | tf_op jit(solution)/shard_map/all_to_all | solution.py:277
  19.3 0.0 copy-done.1
  19.3 0.6 fusion
  20.6 0.0 copy-start.2
  20.6 0.0 copy-start.3
  20.6 0.0 copy-start.5
  20.6 0.6 copy-done.2
  21.3 0.0 copy-done.3
  21.3 0.2 look.1
  21.4 9.4 %all-to-all-done.4 = bf16[64,4,256]{2,1,0:T(4,128)(2,1)S(1)} async-done(((bf16[64,4,256]{2,1,0:T(4,128)(2,1)}), bf16[64,4,256]{2,1,0:T(4,128)(2,1)S(1)}, u32[]{:S(2)}, u32[]{:S(2)}) %all-to-all-start.4) | async-done | bytes 131104 | tf_op jit(solution)/shard_map/all_to_all | solution.py:277
  30.9 0.0 copy-done.4
  30.9 0.0 copy-done.5
  30.9 39.5 %conditional.1 = (bf16[128,1024]{1,0:T(8,128)(2,1)S(1)}, bf16[128,1024]{1,0:T(8,128)(2,1)S(1)}, bf16[256,256]{1,0:T(8,128)(2,1)S(1)}) conditional(s32[]{:T(128)} %convert_element_type.3, (f32[8,256]{1,0:T(8,128)S(1)}, f32[1,128]{1,0:T(1,128)S(1)}, bf16[256,256]{1,0:T(8,128)(2,1)S(1)}, f32[1,128]{1,0:T(1,128)S(1)}, bf16[128,1024]{1,0:T(8,128)(2,1)S(1)}, ...), branch_computations={%region_1.2_spmd, %region_2.3_spmd} | conditional | flops 1611792384 | bytes 13631656 | solution.py:305
  30.9 1.0 %route_kernel.3 = bf16[8,128,256]{2,1,0:T(8,128)(2,1)} custom-call(f32[8,256]{1,0:T(8,128)S(1)} %get-tuple-element.36.plane_ref, f32[1,128]{1,0:T(1,128)S(1)} %get-tuple-element.37.gain_ref, bf16[256,256]{1,0:T(8,128)(2,1)S(1)} %get-tuple-element.38.column_ref), custom_call_target="tpu_custom_call" | custom-call | tf_op jit(solution)/shard_map/cond/branch_1_fun/route_kernel/pallas_call | solution.py:254
  31.9 6.4 %all-to-all-start.2 = ((bf16[8,128,256]{2,1,0:T(8,128)(2,1)}), bf16[8,128,256]{2,1,0:T(8,128)(2,1)S(1)}, u32[]{:S(2)}, u32[]{:S(2)}) async-start(bf16[8,128,256]{2,1,0:T(8,128)(2,1)} %route_kernel.3), calls=%async_computation.2 | async-start | bytes 1048576 | tf_op jit(solution)/shard_map/cond/branch_1_fun/all_to_all | solution.py:287
  38.4 1.9 %collective-permute-start = (bf16[2,64,1024]{2,1,0:T(8,128)(2,1)S(1)}, bf16[2,64,1024]{2,1,0:T(8,128)(2,1)S(1)}, u32[]{:S(2)}, u32[]{:S(2)}) collective-permute-start(bf16[2,64,1024]{2,1,0:T(8,128)(2,1)S(1)} %pad_maximum_fusion), channel_id=1, source_target_pairs={{0,504},{8,0},{16,8},{24,16},{32,24},{40,32},{48,40},{56,48},{64,5... | collective-permute-start | bytes 786440 | tf_op jit(solution)/shard_map/cond/branch_1_fun/ppermute | solution.py:283
  40.3 9.0 %collective-permute-done.refs_0_ = bf16[2,64,1024]{2,1,0:T(8,128)(2,1)S(1)} collective-permute-done((bf16[2,64,1024]{2,1,0:T(8,128)(2,1)S(1)}, bf16[2,64,1024]{2,1,0:T(8,128)(2,1)S(1)}, u32[]{:S(2)}, u32[]{:S(2)}) %collective-permute-start) | collective-permute-done | bytes 262176 | tf_op jit(solution)/shard_map/cond/branch_1_fun/ppermute | solution.py:283
  49.3 0.0 all-to-all-done.2.refs_1_
  49.3 5.1 %attention.3 = (bf16[128,1024]{1,0:T(8,128)(2,1)S(1)}, bf16[128,1024]{1,0:T(8,128)(2,1)S(1)}, bf16[2,64,1024]{2,1,0:T(8,128)(2,1)S(1)}, bf16[8,128,256]{2,1,0:T(8,128)(2,1)}) custom-call(f32[1,128]{1,0:T(1,128)S(1)} %get-tuple-element.33.info_ref, bf16[128,1024]{1,0:T(8,128)(2,1)S(1)} %get-tuple-element.34.query_ref, ...), custom_call_target="tpu_custom_call" | custom-call | flops 1610612736 | bytes 5242880 | tf_op jit(solution)/shard_map/cond/branch_1_fun/attention/pallas_call | solution.py:117
  54.3 1.9 %collective-permute-start.1 = (bf16[2,64,1024]{2,1,0:T(8,128)(2,1)S(1)}, bf16[2,64,1024]{2,1,0:T(8,128)(2,1)S(1)}, u32[]{:S(2)}, u32[]{:S(2)}) collective-permute-start(bf16[2,64,1024]{2,1,0:T(8,128)(2,1)S(1)} %get-tuple-element.39), channel_id=1, source_target_pairs={{0,8},{8,16},{16,24},{24,32},{32,40},{40,48},{48,56},{56,64},{64,7... | collective-permute-start | bytes 786440 | tf_op jit(solution)/shard_map/cond/branch_1_fun/ppermute | solution.py:283
  56.3 4.5 %all-to-all-start.3 = ((bf16[8,128,256]{2,1,0:T(8,128)(2,1)}), bf16[8,128,256]{2,1,0:T(8,128)(2,1)S(1)}, u32[]{:S(2)}, u32[]{:S(2)}) async-start(bf16[8,128,256]{2,1,0:T(8,128)(2,1)} %get-tuple-element.42), calls=%async_computation.3 | async-start | bytes 1048576 | tf_op jit(solution)/shard_map/cond/branch_1_fun/all_to_all | solution.py:290
  60.8 0.0 collective-permute-done.1
  60.9 9.2 %all-to-all-done.3.got_ref = bf16[8,128,256]{2,1,0:T(8,128)(2,1)S(1)} async-done(((bf16[8,128,256]{2,1,0:T(8,128)(2,1)}), bf16[8,128,256]{2,1,0:T(8,128)(2,1)S(1)}, u32[]{:S(2)}, u32[]{:S(2)}) %all-to-all-start.3) | async-done | bytes 524320 | tf_op jit(solution)/shard_map/cond/branch_1_fun/all_to_all | solution.py:290
  70.1 0.2 collect_kernel.3
  70.4 0.0 copy-start.6
  70.4 0.0 copy-start.7
  70.4 15.4 %all_to_all.28.got_ref = bf16[64,4,256]{2,1,0:T(4,128)(2,1)S(1)} all-to-all(bf16[64,4,256]{2,1,0:T(4,128)(2,1)S(1)} %reshape.25), channel_id=1, replica_groups=mesh['z'=8,'x'=4,'c'=2,'tp'=8] {'z','tp'}, dimensions={0} | all-to-all | bytes 262144 | tf_op jit(solution)/shard_map/all_to_all | solution.py:308
  85.9 0.0 copy-done.6
  85.9 0.0 copy-done.7
  85.9 0.7 finish.1
  (9 shorter events, 0.2 us)
Async XLA Ops:
  0.6 0.7 copy-start
  2.0 17.3 %copy-start.1 = (s32[128]{0:T(128)S(1)}, s32[128]{0:T(128)}, u32[]{:S(2)}) copy-start(s32[128]{0:T(128)} %param.12) | copy-start | bytes 1540
  2.0 28.9 %copy-start.4 = (bf16[128,1024]{1,0:T(8,128)(2,1)S(1)}, bf16[128,1024]{1,0:T(8,128)(2,1)}, u32[]{:S(2)}) copy-start(bf16[128,1024]{1,0:T(8,128)(2,1)} %param.8) | copy-start | bytes 786436
  2.0 28.8 %all-to-all-start.4 = ((bf16[64,4,256]{2,1,0:T(4,128)(2,1)}), bf16[64,4,256]{2,1,0:T(4,128)(2,1)S(1)}, u32[]{:S(2)}, u32[]{:S(2)}) async-start(bf16[64,4,256]{2,1,0:T(4,128)(2,1)} %get-tuple-element.57), calls=%async_computation.4 | async-start | bytes 262144 | tf_op jit(solution)/shard_map/all_to_all | solution.py:277
  20.6 0.7 copy-start.2
  20.6 0.7 copy-start.3
  20.6 10.3 %copy-start.5 = (bf16[128,1024]{1,0:T(8,128)(2,1)S(1)}, bf16[128,1024]{1,0:T(8,128)(2,1)}, u32[]{:S(2)}) copy-start(bf16[128,1024]{1,0:T(8,128)(2,1)} %param.11) | copy-start | bytes 786436
  31.9 17.4 %all-to-all-start.2 = ((bf16[8,128,256]{2,1,0:T(8,128)(2,1)}), bf16[8,128,256]{2,1,0:T(8,128)(2,1)S(1)}, u32[]{:S(2)}, u32[]{:S(2)}) async-start(bf16[8,128,256]{2,1,0:T(8,128)(2,1)} %route_kernel.3), calls=%async_computation.2 | async-start | bytes 1048576 | tf_op jit(solution)/shard_map/cond/branch_1_fun/all_to_all | solution.py:287
  38.4 10.9 %collective-permute-start = (bf16[2,64,1024]{2,1,0:T(8,128)(2,1)S(1)}, bf16[2,64,1024]{2,1,0:T(8,128)(2,1)S(1)}, u32[]{:S(2)}, u32[]{:S(2)}) collective-permute-start(bf16[2,64,1024]{2,1,0:T(8,128)(2,1)S(1)} %pad_maximum_fusion), channel_id=1, source_target_pairs={{0,504},{8,0},{16,8},{24,16},{32,24},{40,32},{48,40},{56,48},{64,5... | collective-permute-start | bytes 786440 | tf_op jit(solution)/shard_map/cond/branch_1_fun/ppermute | solution.py:283
  54.3 6.5 %collective-permute-start.1 = (bf16[2,64,1024]{2,1,0:T(8,128)(2,1)S(1)}, bf16[2,64,1024]{2,1,0:T(8,128)(2,1)S(1)}, u32[]{:S(2)}, u32[]{:S(2)}) collective-permute-start(bf16[2,64,1024]{2,1,0:T(8,128)(2,1)S(1)} %get-tuple-element.39), channel_id=1, source_target_pairs={{0,8},{8,16},{16,24},{24,32},{32,40},{40,48},{48,56},{56,64},{64,7... | collective-permute-start | bytes 786440 | tf_op jit(solution)/shard_map/cond/branch_1_fun/ppermute | solution.py:283
  56.3 13.9 %all-to-all-start.3 = ((bf16[8,128,256]{2,1,0:T(8,128)(2,1)}), bf16[8,128,256]{2,1,0:T(8,128)(2,1)S(1)}, u32[]{:S(2)}, u32[]{:S(2)}) async-start(bf16[8,128,256]{2,1,0:T(8,128)(2,1)} %get-tuple-element.42), calls=%async_computation.3 | async-start | bytes 1048576 | tf_op jit(solution)/shard_map/cond/branch_1_fun/all_to_all | solution.py:290
  70.4 15.5 %copy-start.6 = (bf16[128,1024]{1,0:T(8,128)(2,1)}, bf16[128,1024]{1,0:T(8,128)(2,1)S(1)}, u32[]{:S(2)}) copy-start(bf16[128,1024]{1,0:T(8,128)(2,1)S(1)} %get-tuple-element.52) | copy-start | bytes 786436
  70.4 15.5 %copy-start.7 = (bf16[128,1024]{1,0:T(8,128)(2,1)}, bf16[128,1024]{1,0:T(8,128)(2,1)S(1)}, u32[]{:S(2)}) copy-start(bf16[128,1024]{1,0:T(8,128)(2,1)S(1)} %get-tuple-element.53) | copy-start | bytes 786436
